TPU v7x, 128 devices: a whole 4x4x4 slice. The times are simulated.
128 devices in a mesh: dp: 2 (over x_lo), expert: 32 (over z, y, core), mp: 2 (over x_hi).
Axes of the slice: x: 4 (x_hi: 2, x_lo: 2; x = x_hi * 2 + x_lo), y: 4, z: 4, core: 2. Of those that a mesh axis runs over, the one named last changes fastest.
Arguments:
- tokens: bfloat16 [8192, 768], P(('dp', 'expert')), may hold values from -6 to 6
- cotangent: bfloat16 [8192, 768], P(('dp', 'expert')), may hold values from -6 to 6
- routes: int32 [8192, 2], P(('dp', 'expert')), may hold values from 0 to 63, all different within a row; in each aligned block of 128 rows (0 to 127, 128 to 255, ...) at most 6 rows name the same one
- gate_weights: float32 [8192, 2], P(('dp', 'expert')), may hold values from 0.5 to 1
- segments: int32 [64, 128], P(('dp', 'expert')), may hold values from 0 to 3, never falling along the last dimension, each value on 1 to 64 neighbouring positions
- buckets: int32 [128, 128], replicated, may hold values from 0 to 31
- norm_gains: bfloat16 [2, 2, 768], P(None, None, ('dp', 'expert')), may hold values from 0.5 to 1.5
- attention_in: bfloat16 [2, 768, 3, 768], P(None, ('dp', 'expert'), None, 'mp'), may hold values from -0.21875 to 0.21875
- attention_out: bfloat16 [2, 768, 768], P(None, 'mp', ('dp', 'expert')), may hold values from -0.875 to 0.875
- tables: float32 [2, 12, 32], P(None, 'mp'), may hold values from -4 to 4
- dense_in: bfloat16 [768, 2, 3072], P(('dp', 'expert'), None, 'mp'), may hold values from -0.21875 to 0.21875
- dense_out: bfloat16 [3072, 768], P('mp', ('dp', 'expert')), may hold values from -0.109375 to 0.109375
- expert_in: bfloat16 [64, 768, 2, 3072], P('expert', 'dp', None, 'mp'), may hold values from -0.21875 to 0.21875
- expert_out: bfloat16 [64, 3072, 768], P('expert', 'mp', 'dp'), may hold values from -0.4375 to 0.4375
Outputs:
- block_out: bfloat16 [8192, 768], P(('dp', 'expert'))
- tokens_grad: bfloat16 [8192, 768], P(('dp', 'expert'))
- norm_gains_grad: float32 [2, 2, 768], P(None, None, ('dp', 'expert'))
- attention_in_grad: float32 [2, 768, 3, 768], P(None, ('dp', 'expert'), None, 'mp')
- attention_out_grad: float32 [2, 768, 768], P(None, 'mp', ('dp', 'expert'))
- tables_grad: float32 [2, 12, 32], P(None, 'mp')
- dense_in_grad: float32 [768, 2, 3072], P(('dp', 'expert'), None, 'mp')
- dense_out_grad: float32 [3072, 768], P('mp', ('dp', 'expert'))
- expert_in_grad: float32 [64, 768, 2, 3072], P('expert', 'dp', None, 'mp')
- expert_out_grad: float32 [64, 3072, 768], P('expert', 'mp', 'dp')
Inputs may be any that keep to these rules, and one draw needn't show every extreme that they name: `routes`: the 128 tokens of one sequence name no expert more than 6 times in all, a bound that some block reaches; a token's two experts differ. `segments`: along a sequence the numbers never fall.
All inputs are finite; a program needn't handle non-finite values.
Results may differ from a plain program's by a relative error of at most 0.025.
Values may be sent and summed in bfloat16 or wider, within the bound.
No kernel may reach another device: no remote copies, remote signals or barrier semaphores. Data moves between devices by JAX's collectives and lax.ppermute only.
A program may use at most 192 MiB of HBM per device.

v0:
```python
import math

import jax
import jax.numpy as jnp
from jax import lax
from jax.sharding import PartitionSpec as P

HDIM = 64


highest = lax.Precision.HIGHEST
masked_fill = -1000000000.0
epsilon = 1e-06


def from_everyone(value, axis):
    copies = jnp.broadcast_to(value, (lax.axis_size(axis), *value.shape))
    return lax.all_to_all(copies, axis, split_axis=0, concat_axis=0, tiled=True)


def of_everyone(value, axis):
    everything = from_everyone(value, axis)
    return jnp.sum(everything, axis=0)


def side_by_side(arrays, axis, dim, along):
    widths = [math.prod(a.shape[along:]) for a in arrays]
    both = jnp.concatenate(
        [a.reshape(*a.shape[:along], w) for a, w in zip(arrays, widths)], axis=along
    )
    filled = lax.all_gather(both, axis, axis=dim, tiled=True)
    pieces = jnp.split(filled, [sum(widths[:k]) for k in range(1, len(widths))], axis=along)
    return tuple(
        (b.reshape(*filled.shape[:along], *a.shape[along:]) for a, b in zip(arrays, pieces))
    )


def turned_gather(arrays, axis, dims):
    turned = [jnp.moveaxis(a, dim, 0) for a, dim in zip(arrays, dims)]
    widths = [t[0].size for t in turned]
    both = jnp.concatenate([t.reshape(-1, w) for t, w in zip(turned, widths)], axis=1)
    filled = lax.all_gather(both, axis, axis=0, tiled=True)
    pieces = jnp.split(filled, [sum(widths[:k]) for k in range(1, len(widths))], axis=1)
    return tuple(
        (
            jnp.moveaxis(b.reshape(-1, *t.shape[1:]), 0, dim)
            for b, t, dim in zip(pieces, turned, dims)
        )
    )


def product(pattern, first_op, second_op):
    return jnp.einsum(pattern, first_op, second_op, preferred_element_type=jnp.float32)


def across_heads(partial_sum):
    return of_everyone(partial_sum, "mp")


def norm_forward(hidden, norm_gain):
    factor = lax.rsqrt(jnp.mean(hidden * hidden, axis=-1, keepdims=True) + epsilon)
    return ((hidden * factor * norm_gain).astype(jnp.bfloat16), factor)


def norm_backward(hidden, factor, norm_gain, normed_grad):
    scaled = normed_grad * norm_gain
    gain_grad = jnp.sum(normed_grad * hidden * factor, axis=0)
    middle = jnp.mean(hidden * scaled, axis=-1, keepdims=True)
    return (factor * scaled - hidden * (factor * factor * factor) * middle, gain_grad)


def gated_grads(gate_part, up_part, inner_grad):
    unused_out, pullback = jax.vjp(
        lambda gate_value, up_value: jax.nn.gelu(gate_value) * up_value, gate_part, up_part
    )
    return pullback(inner_grad)


def score_block(queries, keys_all, bias_table, allowed, onehot):
    raw_scores = product("qhd,khd->hqk", queries, keys_all)
    bias = jnp.einsum("qkb,hb->hqk", onehot, bias_table, precision=highest)
    return jnp.where(allowed[None], raw_scores * HDIM ** (-0.5) + bias, masked_fill)


def attention_forward(hidden, norm_gain, weight_in, weight_out, bias_table, allowed, onehot):
    seq_len = hidden.shape[0]
    heads_local = bias_table.shape[0]
    normed_low, factor = norm_forward(hidden, norm_gain)
    project = product("sd,dkh->skh", normed_low, weight_in).astype(jnp.bfloat16)
    split_heads = project.reshape(seq_len, 3, heads_local, HDIM)
    scores = score_block(split_heads[:, 0], split_heads[:, 1], bias_table, allowed, onehot)
    row_max = jnp.max(scores, axis=-1, keepdims=True)
    log_total = row_max + jnp.log(jnp.sum(jnp.exp(scores - row_max), axis=-1, keepdims=True))
    weights = jnp.exp(scores - log_total).astype(jnp.bfloat16)
    mixed_heads = product("hqk,khd->qhd", weights, split_heads[:, 2])
    mixed_heads = mixed_heads.astype(jnp.bfloat16).reshape(seq_len, heads_local * HDIM)
    branch = across_heads(jnp.dot(mixed_heads, weight_out, preferred_element_type=jnp.float32))
    return (hidden + branch, (hidden, factor, normed_low, split_heads, log_total, mixed_heads))


def attention_backward(
    upstream, saved_state, norm_gain, weight_in, weight_out, bias_table, allowed, onehot
):
    hidden, factor, normed_low, split_heads, log_total, mixed_heads = saved_state
    seq_len = hidden.shape[0]
    heads_local = bias_table.shape[0]
    branch_grad = upstream.astype(jnp.bfloat16)
    out_grad = product("sh,sd->hd", mixed_heads, branch_grad)
    mixed_grad = product("sd,hd->sh", branch_grad, weight_out)
    mixed_grad = mixed_grad.astype(jnp.bfloat16).reshape(seq_len, heads_local, HDIM)
    queries = split_heads[:, 0]
    keys_all = split_heads[:, 1]
    values_all = split_heads[:, 2]
    weights = jnp.exp(score_block(queries, keys_all, bias_table, allowed, onehot) - log_total)
    values_grad = product("hqk,qhd->khd", weights.astype(jnp.bfloat16), mixed_grad)
    weights_grad = product("qhd,khd->hqk", mixed_grad, values_all)
    scores_grad = weights * (weights_grad - jnp.sum(weights * weights_grad, axis=-1, keepdims=True))
    table_grad = jnp.einsum("hqk,qkb->hb", scores_grad, onehot, precision=highest)
    raw_grad = (scores_grad * HDIM ** (-0.5)).astype(jnp.bfloat16)
    queries_grad = product("hqk,khd->qhd", raw_grad, keys_all)
    keys_grad = product("hqk,qhd->khd", raw_grad, queries)
    project_grad = jnp.stack((queries_grad, keys_grad, values_grad), axis=1).astype(jnp.bfloat16)
    project_grad = project_grad.reshape(seq_len, 3, heads_local * HDIM)
    in_grad = product("sd,skh->dkh", normed_low, project_grad)
    normed_grad = across_heads(product("skh,dkh->sd", project_grad, weight_in))
    hidden_grad, gain_grad = norm_backward(hidden, factor, norm_gain, normed_grad)
    return (upstream + hidden_grad, gain_grad, in_grad, out_grad, table_grad)


def dense_forward(hidden, norm_gain, weight_in, weight_out):
    normed_low, factor = norm_forward(hidden, norm_gain)
    gate_up = product("sd,dkf->skf", normed_low, weight_in)
    inner_act = (jax.nn.gelu(gate_up[:, 0]) * gate_up[:, 1]).astype(jnp.bfloat16)
    branch = across_heads(jnp.dot(inner_act, weight_out, preferred_element_type=jnp.float32))
    return (hidden + branch, (hidden, factor, normed_low, gate_up, inner_act))


def dense_backward(upstream, saved_state, norm_gain, weight_in, weight_out):
    hidden, factor, normed_low, gate_up, inner_act = saved_state
    branch_grad = upstream.astype(jnp.bfloat16)
    out_grad = product("sf,sd->fd", inner_act, branch_grad)
    inner_grad = product("sd,fd->sf", branch_grad, weight_out)
    gate_grad, up_grad = gated_grads(gate_up[:, 0], gate_up[:, 1], inner_grad)
    gate_up_grad = jnp.stack((gate_grad, up_grad), axis=1).astype(jnp.bfloat16)
    in_grad = product("sd,skf->dkf", normed_low, gate_up_grad)
    normed_grad = across_heads(product("skf,dkf->sd", gate_up_grad, weight_in))
    hidden_grad, gain_grad = norm_backward(hidden, factor, norm_gain, normed_grad)
    return (upstream + hidden_grad, gain_grad, in_grad, out_grad)


def slot_layout(routes, sources, capacity, local_experts):
    flat_routes = routes.reshape(-1)
    expert_ids = jnp.arange(local_experts * sources, dtype=jnp.int32)
    onehot = (flat_routes[:, None] == expert_ids[None, :]).astype(jnp.int32)
    slot_ranks = jnp.sum((jnp.cumsum(onehot, axis=0) - 1) * onehot, axis=1)
    return (
        flat_routes % local_experts * (sources * capacity)
        + flat_routes // local_experts * capacity
        + slot_ranks
    )


def expert_forward(hidden, norm_gain, weight_in, weight_out, routes, gate_weights):
    seq_len, model_width = hidden.shape
    local_experts = weight_in.shape[0]
    sources = lax.axis_size("expert")
    capacity = 3 * seq_len // (local_experts * sources)
    slot_ids = slot_layout(routes, sources, capacity, local_experts)
    normed_low, factor = norm_forward(hidden, norm_gain)
    send_rows = jnp.zeros((local_experts * sources * capacity, model_width), jnp.bfloat16)
    send_rows = send_rows.at[slot_ids].set(jnp.repeat(normed_low, 2, axis=0), unique_indices=True)
    send_rows = send_rows.reshape(local_experts, sources, capacity, model_width)
    expert_rows = lax.all_to_all(send_rows, "expert", split_axis=1, concat_axis=1, tiled=True)
    expert_rows = expert_rows.reshape(local_experts, sources * capacity, model_width)
    gate_up = product("erd,edkf->erkf", expert_rows, weight_in)
    inner_act = (jax.nn.gelu(gate_up[:, :, 0]) * gate_up[:, :, 1]).astype(jnp.bfloat16)
    expert_result = across_heads(product("erf,efd->erd", inner_act, weight_out)).astype(
        jnp.bfloat16
    )
    returned = lax.all_to_all(
        expert_result.reshape(local_experts, sources, capacity, model_width),
        "expert",
        split_axis=1,
        concat_axis=1,
        tiled=True,
    )
    picked = returned.reshape(-1, model_width)[slot_ids].reshape(seq_len, 2, model_width)
    mixture = jnp.sum(picked.astype(jnp.float32) * gate_weights[:, :, None], axis=1)
    return (hidden + mixture, (hidden, factor, slot_ids, expert_rows, gate_up, inner_act))


def expert_backward(upstream, saved_state, norm_gain, weight_in, weight_out, gate_weights):
    hidden, factor, slot_ids, expert_rows, gate_up, inner_act = saved_state
    seq_len, model_width = hidden.shape
    local_experts = expert_rows.shape[0]
    row_count = expert_rows.shape[1]
    sources = lax.axis_size("expert")
    slot_grad = (jnp.repeat(upstream, 2, axis=0) * gate_weights.reshape(-1, 1)).astype(jnp.bfloat16)
    send_grad = (
        jnp.zeros((local_experts * row_count, model_width), jnp.bfloat16)
        .at[slot_ids]
        .set(slot_grad, unique_indices=True)
    )
    send_grad = send_grad.reshape(local_experts, sources, row_count // sources, model_width)
    rows_grad = lax.all_to_all(send_grad, "expert", split_axis=1, concat_axis=1, tiled=True)
    rows_grad = rows_grad.reshape(local_experts, row_count, model_width)
    inner_grad = product("erd,efd->erf", rows_grad, weight_out)
    gate_grad, up_grad = gated_grads(gate_up[:, :, 0], gate_up[:, :, 1], inner_grad)
    gate_up_grad = jnp.stack((gate_grad, up_grad), axis=2).astype(jnp.bfloat16)
    half_width = model_width // lax.axis_size("dp")
    half_start = lax.axis_index("dp") * half_width
    inner_piece, gate_piece, rows_piece, grad_piece = side_by_side(
        (inner_act, gate_up_grad, expert_rows, rows_grad), "dp", 1, 2
    )
    rows_mine = lax.dynamic_slice_in_dim(rows_piece, half_start, half_width, 2)
    grad_mine = lax.dynamic_slice_in_dim(grad_piece, half_start, half_width, 2)
    in_grad = product("erd,erkf->edkf", rows_mine, gate_piece)
    out_grad = product("erf,erd->efd", inner_piece, grad_mine)
    rows_back = across_heads(product("erkf,edkf->erd", gate_up_grad, weight_in))
    returned = lax.all_to_all(
        rows_back.reshape(local_experts, sources, row_count // sources, model_width).astype(
            jnp.bfloat16
        ),
        "expert",
        split_axis=1,
        concat_axis=1,
        tiled=True,
    ).astype(jnp.float32)
    normed_grad = jnp.sum(
        returned.reshape(-1, model_width)[slot_ids].reshape(seq_len, 2, model_width), axis=1
    )
    hidden_grad, gain_grad = norm_backward(hidden, factor, norm_gain, normed_grad)
    return (upstream + hidden_grad, gain_grad, in_grad, out_grad)


def body(
    tokens,
    cotangent,
    routes,
    gate_weights,
    segments,
    buckets,
    norm_gains,
    attention_in,
    attention_out,
    tables,
    dense_in,
    dense_out,
    expert_in,
    expert_out,
):
    dense_set = (attention_in, attention_out, norm_gains, dense_in, dense_out)
    gathered = turned_gather(
        (dense_set[0], dense_set[1], dense_set[2], dense_set[3], dense_set[4]),
        ("dp", "expert"),
        (1, 2, 2, 0, 1),
    )
    expert_set = turned_gather((expert_in, expert_out), "dp", (1, 2))
    seq_len = tokens.shape[0]
    positions = jnp.arange(seq_len, dtype=jnp.int32)
    segment_row = segments[0]
    allowed = (segment_row[:, None] == segment_row[None, :]) & (
        positions[None, :] <= positions[:, None]
    )
    bucket_ids = jnp.arange(tables.shape[2], dtype=jnp.int32)
    onehot = (buckets[:, :, None] == bucket_ids[None, None, :]).astype(jnp.float32)
    full_in, full_out, full_gains, full_dense_in, full_dense_out = gathered
    gains_float = full_gains.astype(jnp.float32)
    hidden = tokens.astype(jnp.float32)
    hidden, first_state = attention_forward(
        hidden, gains_float[0, 0], full_in[0], full_out[0], tables[0], allowed, onehot
    )
    hidden, dense_state = dense_forward(hidden, gains_float[0, 1], full_dense_in, full_dense_out)
    hidden, second_state = attention_forward(
        hidden, gains_float[1, 0], full_in[1], full_out[1], tables[1], allowed, onehot
    )
    hidden, expert_state = expert_forward(
        hidden, gains_float[1, 1], expert_set[0], expert_set[1], routes, gate_weights
    )
    block_out = hidden.astype(jnp.bfloat16)
    upstream = cotangent.astype(jnp.float32)
    upstream, gain_moe, expert_in_grad, expert_out_grad = expert_backward(
        upstream, expert_state, gains_float[1, 1], expert_set[0], expert_set[1], gate_weights
    )
    upstream, gain_second, in_second, out_second, table_second = attention_backward(
        upstream,
        second_state,
        gains_float[1, 0],
        full_in[1],
        full_out[1],
        tables[1],
        allowed,
        onehot,
    )
    upstream, gain_dense, dense_in_grad, dense_out_grad = dense_backward(
        upstream, dense_state, gains_float[0, 1], full_dense_in, full_dense_out
    )
    upstream, gain_first, in_first, out_first, table_first = attention_backward(
        upstream,
        first_state,
        gains_float[0, 0],
        full_in[0],
        full_out[0],
        tables[0],
        allowed,
        onehot,
    )
    gains_grad = jnp.stack(
        (jnp.stack((gain_first, gain_dense)), jnp.stack((gain_second, gain_moe)))
    )
    dense_grads = (
        lax.psum_scatter(
            jnp.stack((in_first, in_second)), ("dp", "expert"), scatter_dimension=1, tiled=True
        ),
        lax.psum_scatter(
            jnp.stack((out_first, out_second)), ("dp", "expert"), scatter_dimension=2, tiled=True
        ),
        lax.psum_scatter(gains_grad, ("dp", "expert"), scatter_dimension=2, tiled=True),
        lax.psum_scatter(dense_in_grad, ("dp", "expert"), scatter_dimension=0, tiled=True),
        lax.psum_scatter(dense_out_grad, ("dp", "expert"), scatter_dimension=1, tiled=True),
    )
    tables_grad = of_everyone(jnp.stack((table_first, table_second)), ("dp", "expert"))
    return (
        block_out,
        upstream.astype(jnp.bfloat16),
        dense_grads[2],
        dense_grads[0],
        dense_grads[1],
        tables_grad,
        dense_grads[3],
        dense_grads[4],
        expert_in_grad,
        expert_out_grad,
    )


def solution(mesh):
    placed = (
        P(("dp", "expert"), None),
        P(("dp", "expert"), None),
        P(("dp", "expert"), None),
        P(("dp", "expert"), None),
        P(("dp", "expert"), None),
        P(),
        P(None, None, ("dp", "expert")),
        P(None, ("dp", "expert"), None, "mp"),
        P(None, "mp", ("dp", "expert")),
        P(None, "mp", None),
        P(("dp", "expert"), None, "mp"),
        P("mp", ("dp", "expert")),
        P("expert", "dp", None, "mp"),
        P("expert", "mp", "dp"),
    )
    return jax.shard_map(
        body,
        mesh=mesh,
        in_specs=placed,
        out_specs=(
            P(("dp", "expert"), None),
            P(("dp", "expert"), None),
            P(None, None, ("dp", "expert")),
            P(None, ("dp", "expert"), None, "mp"),
            P(None, "mp", ("dp", "expert")),
            P(None, "mp", None),
            P(("dp", "expert"), None, "mp"),
            P("mp", ("dp", "expert")),
            P("expert", "dp", None, "mp"),
            P("expert", "mp", "dp"),
        ),
        check_vma=False,
    )
```

profile of v0, /device:TPU:1, one launch (start us, length us, event | category | flops | bytes accessed | tf_op | source)
XLA Modules:
  0.0 1230.2 jit_solution(5981418415715219963)
XLA Ops:
  12.4 12.6 %copy.437 = bf16[2,384,2,1536]{1,3,2,0:T(8,128)(2,1)} copy(bf16[2,384,2,1536]{3,2,1,0:T(2,128)(2,1)} %param.26) | data formatting | bytes 9437184 | tf_op args[12]
  25.0 12.7 %pad_maximum_fusion = bf16[384,9216]{0,1:T(8,128)(2,1)} fusion(bf16[384,3072]{0,1:T(8,128)(2,1)S(1)} %bitcast.334, bf16[384,6144]{0,1:T(8,128)(2,1)} %bitcast.307), kind=kLoop, calls=%fused_computation.8 | loop fusion | flops 14155776 | bytes 14155776 | tf_op jit(solution)/shard_map/concatenate | solution.py:41
  41.6 97.3 %all-gather.9.cloned.1.call-done = bf16[64,12,7684]{2,1,0:T(8,128)(2,1)} async-done(((bf16[1,12,7684]{2,1,0:T(8,128)(2,1)}), bf16[64,12,7684]{2,1,0:T(8,128)(2,1)}) %all-gather.9.cloned.1.call-update) | async-done | bytes 11802640 | tf_op jit(solution)/shard_map/all_gather | solution.py:42
  138.9 18.7 %reshape.490 = bf16[768,7684]{1,0:T(8,128)(2,1)} reshape(bf16[64,12,7684]{2,1,0:T(8,128)(2,1)} %all-gather.9.cloned.1.call-done) | data formatting | bytes 23605248
  157.6 4.4 split.45
  165.2 4.6 copy.418
  169.9 3.6 copy.419
  179.6 3.7 all-to-all-start
  184.2 6.7 split.47
  190.9 6.7 copy.426
  197.7 6.7 all-to-all-done
  205.7 4.0 fusion.104
  210.0 3.1 fusion.20
  214.1 3.5 all-to-all-start.1
  220.4 17.9 %all-to-all-done.1 = f32[2,128,768]{2,1,0:T(8,128)S(1)} async-done(((f32[2,128,768]{2,1,0:T(8,128)}), f32[2,128,768]{2,1,0:T(8,128)S(1)}, u32[]{:S(2)}, u32[]{:S(2)}) %all-to-all-start.1) | async-done | bytes 786464 | tf_op jit(solution)/shard_map/all_to_all | solution.py:18
  244.2 3.5 all-to-all-start.2
  261.1 3.2 scatter_custom_fusion.1
  269.0 8.1 all-to-all-start.6
  289.2 5.4 all-to-all-start.3
  296.6 40.5 %all-gather.5.cloned.1.call-done = bf16[768,9216]{0,1:T(8,128)(2,1)} async-done(((bf16[384,9216]{0,1:T(8,128)(2,1)}), bf16[768,9216]{0,1:T(8,128)(2,1)}) %all-gather.5.cloned.1.call-update) | async-done | bytes 14155792 | tf_op jit(solution)/shard_map/all_gather | solution.py:42
  337.1 8.0 split.49
  345.1 12.6 %copy.438 = bf16[768,2,2,1536]{3,0,2,1:T(8,128)(2,1)} copy(bf16[768,2,2,1536]{0,3,2,1:T(8,128)(2,1)} %bitcast.300) | data formatting | bytes 18874368 | tf_op jit(solution)/shard_map/reshape | solution.py:46
  357.7 4.8 split.50
  363.5 5.8 fusion.3
  369.4 6.4 fusion.11
  379.5 5.1 all-to-all-start.7
  391.3 21.9 %all-to-all-done.7 = f32[2,2,192,768]{3,2,1,0:T(8,128)} async-done(((f32[2,2,192,768]{3,2,1,0:T(8,128)}), f32[2,2,192,768]{3,2,1,0:T(8,128)}, u32[]{:S(2)}, u32[]{:S(2)}) %all-to-all-start.7) | async-done | bytes 2359328 | tf_op jit(solution)/shard_map/all_to_all | solution.py:18
  414.8 5.2 all-to-all-start.4
  420.1 5.0 pad_maximum_fusion.2
  425.1 9.4 copy.478
  437.9 9.9 all-to-all-done.4
  447.8 9.5 all-to-all-start.8
  460.8 8.7 all-to-all-done.8
  469.5 5.3 all-to-all-start.5
  484.3 2.8 all-to-all-done.5
  507.4 4.4 all-to-all-start.9
  515.8 17.1 %all-to-all-done.9 = f32[2,128,768]{2,1,0:T(8,128)} async-done(((f32[2,128,768]{2,1,0:T(8,128)}), f32[2,128,768]{2,1,0:T(8,128)}, u32[]{:S(2)}, u32[]{:S(2)}) %all-to-all-start.9) | async-done | bytes 786464 | tf_op jit(solution)/shard_map/all_to_all | solution.py:18
  537.3 3.3 fusion.72
  542.4 4.3 all-to-all-start.10
  548.5 22.1 %copy.474 = f32[768,2,1536]{2,1,0:T(2,128)} copy(f32[768,2,1536]{2,0,1:T(8,128)S(1)} %fusion.58) | data formatting | bytes 18874368 | tf_op jit(solution)/shard_map/sd,skf->dkf/dot_general | solution.py:53
  576.6 3.1 copy.469
  581.7 3.4 pad_maximum_fusion.1
  585.1 11.4 copy.468
  598.8 3.0 fusion.86
  601.8 177.0 %fusion = f32[1536,16]{0,1:T(8,128)S(1)} fusion(f32[1536,768]{0,1:T(8,128)} %fusion.86), kind=kCustom, calls=%all-reduce-scatter | all-reduce-scatter fusion | flops 1572865 | bytes 4817408
  786.6 6.1 collective-permute-done.15
  794.0 15.0 %collective-permute-start.9 = (f32[1536,16]{0,1:T(8,128)S(1)}, f32[1536,16]{0,1:T(8,128)S(1)}, u32[]{:S(2)}, u32[]{:S(2)}) collective-permute-start(f32[1536,16]{0,1:T(8,128)S(1)} %fusion), channel_id=1, source_target_pairs={{0,20},{2,22},{4,24},{6,26},{8,28},{10,30},{12,32},{14,34},{16,36}... | collective-permute-start | bytes 294920
  810.3 3.5 collective-permute-start.7
  813.9 2.9 collective-permute-start.6
  816.8 3.5 collective-permute-start.5
  821.4 4.9 all-to-all-start.12
  826.3 4.8 collective-permute-start.4
  831.1 3.4 collective-permute-start.3
  834.5 4.9 collective-permute-start.2
  846.6 4.8 all-to-all-start.11
  853.5 25.2 %concatenate.16 = f32[1536,268]{0,1:T(8,128)} concatenate(f32[1536,12]{0,1:T(8,128)S(1)} %collective-permute-done.15, f32[1536,16]{0,1:T(8,128)S(1)} %collective-permute-done.14, f32[1536,16]{0,1:T(8,128)S(1)} %collective-permute-done.13, f32[1536,16]{0,1:T(8,128)S(1)} %collective-permute-done.12, f32[1536,16]{0,1:T(8,128)S(1)} %collective-permute-done.11, ...), dimensions={1} | concatenate | bytes 3293184
  883.1 269.5 %all-reduce = f32[2,2,768]{2,1,0:T(2,128)S(1)} all-reduce(f32[2,2,768]{2,1,0:T(2,128)S(1)} %pad_maximum_fusion.13), channel_id=2, replica_groups=mesh['dp'=2,'expert'=32,'mp'=2] {'dp','expert'}, use_global_device_ids=true, to_apply=%region_33.34.clone | all-reduce | flops 3072 | bytes 24576
  1154.1 7.8 split.52
  1161.9 12.5 %copy.516 = bf16[2,384,3072]{1,2,0:T(8,128)(2,1)} copy(bf16[2,384,3072]{2,0,1:T(2,128)(2,1)} %split.52) | data formatting | bytes 9437184
  1174.4 3.3 fusion.122
  1179.1 5.0 fusion.51
  1184.1 14.6 %copy.484 = f32[2,384,2,1536]{3,2,1,0:T(2,128)} copy(f32[2,384,2,1536]{3,1,2,0:T(8,128)S(1)} %fusion.51) | data formatting | bytes 18874368
  1200.3 3.8 fusion.12
  1204.2 14.5 %all-reduce.9.cloned.1.call-done = (f32[2,768,3,384]{3,0,2,1:T(2,128)}, f32[2,384,768]{1,0,2:T(2,128)}, f32[768,2,1536]{2,1,0:T(2,128)}) async-done(((f32[2,768,3,384]{3,0,2,1:T(2,128)}, f32[2,384,768]{1,0,2:T(2,128)}, f32[768,2,1536]{2,1,0:T(2,128)}), (f32[2,768,3,384]{3,0,2,1:T(2,128)}, f32[2,384,768]{1,0,2:T(2,128)}, f32[768,2,1536]{2,1,0:T(2,128)})) %all-reduce.9.cloned.1.call-update) | async-done | bytes 18874384
  (395 shorter events, 166.2 us)
Async XLA Ops:
  7.2 131.7 %all-gather.9.cloned.1.call-start = ((), (), s32[]{:S(2)}) async-start(), calls=%async_computation.15 | async-start | bytes 16240640 | tf_op jit(solution)/shard_map/all_gather | solution.py:42
  12.3 12.6 %copy-start.33 = (bf16[2,1536,384]{2,1,0:T(8,128)(2,1)S(1)}, bf16[2,1536,384]{2,1,0:T(8,128)(2,1)}, u32[]{:S(2)}) copy-start(bf16[2,1536,384]{2,1,0:T(8,128)(2,1)} %param.27) | copy-start | bytes 7077892
  12.3 324.8 %all-gather.5.cloned.1.call-start = ((), (), s32[]{:S(2)}) async-start(), calls=%async_computation.13 | async-start | bytes 21233664 | tf_op jit(solution)/shard_map/all_gather | solution.py:42
  38.7 118.9 %copy-start.43 = (s32[128,128]{0,1:T(8,128)}, s32[128,128]{0,1:T(8,128)S(1)}, u32[]{:S(2)}) copy-start(s32[128,128]{0,1:T(8,128)S(1)} %copy.421) | copy-start | bytes 196612
  178.0 13.0 %copy-start.38 = (bf16[6,64,128]{2,1,0:T(8,128)(2,1)}, bf16[6,64,128]{2,1,0:T(8,128)(2,1)S(1)}, u32[]{:S(2)}) copy-start(bf16[6,64,128]{2,1,0:T(8,128)(2,1)S(1)} %convolution_convert_fusion.9) | copy-start | bytes 294916
  179.6 24.7 %all-to-all-start = ((f32[2,128,768]{2,1,0:T(8,128)}), f32[2,128,768]{2,1,0:T(8,128)S(1)}, u32[]{:S(2)}, u32[]{:S(2)}) async-start(f32[2,128,768]{2,1,0:T(8,128)} %broadcast_in_dim.87), calls=%async_computation | async-start | bytes 1572864 | tf_op jit(solution)/shard_map/all_to_all | solution.py:18
  190.9 13.4 %copy-start.14 = (bf16[128,768]{1,0:T(8,128)(2,1)S(1)}, bf16[128,768]{1,0:T(8,128)(2,1)}, u32[]{:S(2)}) copy-start(bf16[128,768]{1,0:T(8,128)(2,1)} %param.14) | copy-start | bytes 589828
  190.9 14.7 %copy-start.55 = (f32[768]{0:T(1024)S(1)}, f32[768]{0:T(1024)}, u32[]{:S(2)}) copy-start(f32[768]{0:T(1024)} %get-tuple-element.90) | copy-start | bytes 9220
  210.0 7.7 copy-start.72
  214.1 24.2 %all-to-all-start.1 = ((f32[2,128,768]{2,1,0:T(8,128)}), f32[2,128,768]{2,1,0:T(8,128)S(1)}, u32[]{:S(2)}, u32[]{:S(2)}) async-start(f32[2,128,768]{2,1,0:T(8,128)} %broadcast_in_dim.88), calls=%async_computation.1 | async-start | bytes 1572864 | tf_op jit(solution)/shard_map/all_to_all | solution.py:18
  217.6 21.4 %copy-start.61 = (f32[768]{0:T(1024)S(1)}, f32[768]{0:T(1024)}, u32[]{:S(2)}) copy-start(f32[768]{0:T(1024)} %get-tuple-element.89) | copy-start | bytes 9220
  238.5 39.4 %copy-start.3 = (f32[128,768]{1,0:T(8,128)}, f32[128,768]{1,0:T(8,128)S(1)}, u32[]{:S(2)}) copy-start(f32[128,768]{1,0:T(8,128)S(1)} %get-tuple-element.98) | copy-start | bytes 1179652
  244.2 24.8 %all-to-all-start.2 = ((f32[2,128,768]{2,1,0:T(8,128)}), f32[2,128,768]{2,1,0:T(8,128)S(1)}, u32[]{:S(2)}, u32[]{:S(2)}) async-start(f32[2,128,768]{2,1,0:T(8,128)} %broadcast_in_dim.89), calls=%async_computation.2 | async-start | bytes 1572864 | tf_op jit(solution)/shard_map/all_to_all | solution.py:18
  261.1 18.9 %copy-start.73 = (s32[256,1]{0,1:T(1,128)}, s32[256,1]{0,1:T(1,128)S(1)}, u32[]{:S(2)}) copy-start(s32[256,1]{0,1:T(1,128)S(1)} %compare_select_fusion) | copy-start | bytes 3076
  266.4 13.2 %copy-start.63 = (f32[768]{0:T(1024)S(1)}, f32[768]{0:T(1024)}, u32[]{:S(2)}) copy-start(f32[768]{0:T(1024)} %get-tuple-element.88) | copy-start | bytes 9220
  269.0 20.2 %all-to-all-start.6 = ((bf16[2,32,6,768]{3,0,2,1:T(2,128)(2,1)}), bf16[2,32,6,768]{3,0,2,1:T(2,128)(2,1)}, u32[]{:S(2)}, u32[]{:S(2)}) async-start(bf16[2,32,6,768]{3,0,2,1:T(2,128)(2,1)} %copy.445), calls=%async_computation.6 | async-start | bytes 1179648 | tf_op jit(solution)/shard_map/all_to_all | solution.py:205
  279.0 8.2 copy-start.9
  289.2 73.3 %all-to-all-start.3 = ((bf16[2,32,6,768]{3,0,2,1:T(2,128)(2,1)}), bf16[2,32,6,768]{3,0,2,1:T(2,128)(2,1)S(1)}, u32[]{:S(2)}, u32[]{:S(2)}) async-start(bf16[2,32,6,768]{3,0,2,1:T(2,128)(2,1)} %copy.436), calls=%async_computation.3 | async-start | bytes 1179648 | tf_op jit(solution)/shard_map/all_to_all | solution.py:173
  363.5 12.3 %slice-start.3 = ((s8[9437184]{0:T(1024)(128)(4,1)}), s8[4194304]{0:T(1024)(128)(4,1)S(1)}, s32[]{:S(2)}) async-start(s8[9437184]{0:T(1024)(128)(4,1)} %bitcast.301), calls=%async_computation.20 | async-start | bytes 8388608
  363.5 12.3 %slice-start.4 = ((s8[9437184]{0:T(1024)(128)(4,1)}), s8[4194304]{0:T(1024)(128)(4,1)S(1)}, s32[]{:S(2)}) async-start(s8[9437184]{0:T(1024)(128)(4,1)} %bitcast.301), calls=%async_computation.21 | async-start | bytes 8388608
  369.4 6.5 slice-start.5
  379.5 8.8 slice-start.6
  379.5 33.7 %all-to-all-start.7 = ((f32[2,2,192,768]{3,2,1,0:T(8,128)}), f32[2,2,192,768]{3,2,1,0:T(8,128)}, u32[]{:S(2)}, u32[]{:S(2)}) async-start(f32[2,2,192,768]{3,2,1,0:T(8,128)} %broadcast_in_dim.93), calls=%async_computation.7 | async-start | bytes 4718592 | tf_op jit(solution)/shard_map/all_to_all | solution.py:18
  414.8 33.0 %all-to-all-start.4 = ((f32[2,2,192,768]{3,2,1,0:T(8,128)}), f32[2,2,192,768]{3,2,1,0:T(8,128)}, u32[]{:S(2)}, u32[]{:S(2)}) async-start(f32[2,2,192,768]{3,2,1,0:T(8,128)} %broadcast_in_dim.91), calls=%async_computation.4 | async-start | bytes 4718592 | tf_op jit(solution)/shard_map/all_to_all | solution.py:18
  420.1 734.1 %all-gather.7.cloned.1.call-start = ((), (), s32[]{:S(2)}) async-start(), calls=%async_computation.14 | async-start | bytes 14155776 | tf_op jit(solution)/shard_map/all_gather | solution.py:31
  447.8 21.8 %all-to-all-start.8 = ((bf16[2,32,6,768]{3,0,2,1:T(2,128)(2,1)}), bf16[2,32,6,768]{3,0,2,1:T(2,128)(2,1)S(1)}, u32[]{:S(2)}, u32[]{:S(2)}) async-start(bf16[2,32,6,768]{3,0,2,1:T(2,128)(2,1)} %bitcast.63), calls=%async_computation.8 | async-start | bytes 1179648 | tf_op jit(solution)/shard_map/all_to_all | solution.py:220
  469.5 17.6 %all-to-all-start.5 = ((bf16[2,32,6,768]{3,0,2,1:T(2,128)(2,1)}), bf16[2,32,6,768]{3,0,2,1:T(2,128)(2,1)}, u32[]{:S(2)}, u32[]{:S(2)}) async-start(bf16[2,32,6,768]{3,0,2,1:T(2,128)(2,1)} %bitcast.56), calls=%async_computation.5 | async-start | bytes 1179648 | tf_op jit(solution)/shard_map/all_to_all | solution.py:180
  499.8 12.0 copy-start.11
  504.2 7.7 copy-start.41
  506.4 6.8 copy-start.4
  506.4 6.8 copy-start.50
  506.4 6.8 copy-start.52
  506.4 6.8 copy-start.62
  506.4 6.8 copy-start.71
  507.4 25.5 %all-to-all-start.9 = ((f32[2,128,768]{2,1,0:T(8,128)}), f32[2,128,768]{2,1,0:T(8,128)}, u32[]{:S(2)}, u32[]{:S(2)}) async-start(f32[2,128,768]{2,1,0:T(8,128)} %broadcast_in_dim.94), calls=%async_computation.9 | async-start | bytes 1572864 | tf_op jit(solution)/shard_map/all_to_all | solution.py:18
  513.2 22.9 %copy-start.12 = (f32[128,768]{1,0:T(8,128)S(1)}, f32[128,768]{1,0:T(8,128)}, u32[]{:S(2)}) copy-start(f32[128,768]{1,0:T(8,128)} %copy-done.11) | copy-start | bytes 1179652
  513.2 22.9 %copy-start.79 = (f32[128]{0:T(128)S(1)}, f32[128]{0:T(128)}, u32[]{:S(2)}) copy-start(f32[128]{0:T(128)} %get-tuple-element.117) | copy-start | bytes 1540
  532.9 7.8 slice-start
  542.4 28.2 %all-to-all-start.10 = ((f32[2,128,768]{2,1,0:T(8,128)}), f32[2,128,768]{2,1,0:T(8,128)}, u32[]{:S(2)}, u32[]{:S(2)}) async-start(f32[2,128,768]{2,1,0:T(8,128)} %broadcast_in_dim.95), calls=%async_computation.10 | async-start | bytes 1572864 | tf_op jit(solution)/shard_map/all_to_all | solution.py:18
  546.8 671.9 %all-reduce.9.cloned.1.call-start = ((), (), s32[]{:S(2)}) async-start(), calls=%async_computation.16 | async-start | bytes 37748736
  548.5 23.5 %copy-start.21 = (f32[128,768]{1,0:T(8,128)S(1)}, f32[128,768]{1,0:T(8,128)}, u32[]{:S(2)}) copy-start(f32[128,768]{1,0:T(8,128)} %copy-done.20) | copy-start | bytes 1179652
  548.5 23.5 %copy-start.78 = (f32[128]{0:T(128)S(1)}, f32[128]{0:T(128)}, u32[]{:S(2)}) copy-start(f32[128]{0:T(128)} %get-tuple-element.115) | copy-start | bytes 1540
  601.8 183.6 %copy-start.26 = (f32[6,128,128]{1,2,0:T(8,128)S(1)}, f32[6,128,128]{1,2,0:T(8,128)}, u32[]{:S(2)}) copy-start(f32[6,128,128]{1,2,0:T(8,128)} %copy-done.25) | copy-start | bytes 1179652
  778.8 15.2 %collective-permute-start.14 = (f32[1536,16]{0,1:T(8,128)S(1)}, f32[1536,16]{0,1:T(8,128)S(1)}, u32[]{:S(2)}, u32[]{:S(2)}) collective-permute-start(f32[1536,16]{0,1:T(8,128)S(1)} %fusion), channel_id=1, source_target_pairs={{0,30},{2,32},{4,34},{6,36},{8,38},{10,40},{12,42},{14,44},{16,46}... | collective-permute-start | bytes 294920
  780.1 28.9 %collective-permute-start.13 = (f32[1536,16]{0,1:T(8,128)S(1)}, f32[1536,16]{0,1:T(8,128)S(1)}, u32[]{:S(2)}, u32[]{:S(2)}) collective-permute-start(f32[1536,16]{0,1:T(8,128)S(1)} %fusion), channel_id=1, source_target_pairs={{0,28},{2,30},{4,32},{6,34},{8,36},{10,38},{12,40},{14,42},{16,44}... | collective-permute-start | bytes 294920
  781.4 28.9 %collective-permute-start.12 = (f32[1536,16]{0,1:T(8,128)S(1)}, f32[1536,16]{0,1:T(8,128)S(1)}, u32[]{:S(2)}, u32[]{:S(2)}) collective-permute-start(f32[1536,16]{0,1:T(8,128)S(1)} %fusion), channel_id=1, source_target_pairs={{0,26},{2,28},{4,30},{6,32},{8,34},{10,36},{12,38},{14,40},{16,42}... | collective-permute-start | bytes 294920
  782.7 31.1 %collective-permute-start.11 = (f32[1536,16]{0,1:T(8,128)S(1)}, f32[1536,16]{0,1:T(8,128)S(1)}, u32[]{:S(2)}, u32[]{:S(2)}) collective-permute-start(f32[1536,16]{0,1:T(8,128)S(1)} %fusion), channel_id=1, source_target_pairs={{0,24},{2,26},{4,28},{6,30},{8,32},{10,34},{12,36},{14,38},{16,40}... | collective-permute-start | bytes 294920
  784.0 8.7 collective-permute-start.15
  792.7 24.0 %collective-permute-start.10 = (f32[1536,16]{0,1:T(8,128)S(1)}, f32[1536,16]{0,1:T(8,128)S(1)}, u32[]{:S(2)}, u32[]{:S(2)}) collective-permute-start(f32[1536,16]{0,1:T(8,128)S(1)} %fusion), channel_id=1, source_target_pairs={{0,22},{2,24},{4,26},{6,28},{8,30},{10,32},{12,34},{14,36},{16,38}... | collective-permute-start | bytes 294920
  794.0 32.3 %collective-permute-start.9 = (f32[1536,16]{0,1:T(8,128)S(1)}, f32[1536,16]{0,1:T(8,128)S(1)}, u32[]{:S(2)}, u32[]{:S(2)}) collective-permute-start(f32[1536,16]{0,1:T(8,128)S(1)} %fusion), channel_id=1, source_target_pairs={{0,20},{2,22},{4,24},{6,26},{8,28},{10,30},{12,32},{14,34},{16,36}... | collective-permute-start | bytes 294920
  809.0 22.1 %collective-permute-start.8 = (f32[1536,16]{0,1:T(8,128)S(1)}, f32[1536,16]{0,1:T(8,128)S(1)}, u32[]{:S(2)}, u32[]{:S(2)}) collective-permute-start(f32[1536,16]{0,1:T(8,128)S(1)} %fusion), channel_id=1, source_target_pairs={{0,18},{2,20},{4,22},{6,24},{8,26},{10,28},{12,30},{14,32},{16,34}... | collective-permute-start | bytes 294920
  810.3 24.2 %collective-permute-start.7 = (f32[1536,16]{0,1:T(8,128)S(1)}, f32[1536,16]{0,1:T(8,128)S(1)}, u32[]{:S(2)}, u32[]{:S(2)}) collective-permute-start(f32[1536,16]{0,1:T(8,128)S(1)} %fusion), channel_id=1, source_target_pairs={{0,16},{2,18},{4,20},{6,22},{8,24},{10,26},{12,28},{14,30},{16,32}... | collective-permute-start | bytes 294920
  813.9 25.6 %collective-permute-start.6 = (f32[1536,16]{0,1:T(8,128)S(1)}, f32[1536,16]{0,1:T(8,128)S(1)}, u32[]{:S(2)}, u32[]{:S(2)}) collective-permute-start(f32[1536,16]{0,1:T(8,128)S(1)} %fusion), channel_id=1, source_target_pairs={{0,14},{2,16},{4,18},{6,20},{8,22},{10,24},{12,26},{14,28},{16,30}... | collective-permute-start | bytes 294920
  816.8 24.9 %collective-permute-start.5 = (f32[1536,16]{0,1:T(8,128)S(1)}, f32[1536,16]{0,1:T(8,128)S(1)}, u32[]{:S(2)}, u32[]{:S(2)}) collective-permute-start(f32[1536,16]{0,1:T(8,128)S(1)} %fusion), channel_id=1, source_target_pairs={{0,12},{2,14},{4,16},{6,18},{8,20},{10,22},{12,24},{14,26},{16,28}... | collective-permute-start | bytes 294920
  821.4 24.3 %all-to-all-start.12 = ((f32[64,1,384]{2,1,0:T(1,128)}), f32[64,1,384]{2,1,0:T(1,128)S(1)}, u32[]{:S(2)}, u32[]{:S(2)}) async-start(f32[64,1,384]{2,1,0:T(1,128)} %reshape.524), calls=%async_computation.12 | async-start | bytes 196608 | tf_op jit(solution)/shard_map/all_to_all | solution.py:18
  826.3 25.2 %copy-start.75 = (u32[128]{0:T(128)S(1)}, u32[128]{0:T(128)}, u32[]{:S(2)}) copy-start(u32[128]{0:T(128)} %constant.99) | copy-start | bytes 1540
  826.3 27.1 %collective-permute-start.4 = (f32[1536,16]{0,1:T(8,128)S(1)}, f32[1536,16]{0,1:T(8,128)S(1)}, u32[]{:S(2)}, u32[]{:S(2)}) collective-permute-start(f32[1536,16]{0,1:T(8,128)S(1)} %fusion), channel_id=1, source_target_pairs={{0,10},{2,12},{4,14},{6,16},{8,18},{10,20},{12,22},{14,24},{16,26}... | collective-permute-start | bytes 294920
  831.1 22.3 %collective-permute-start.3 = (f32[1536,16]{0,1:T(8,128)S(1)}, f32[1536,16]{0,1:T(8,128)S(1)}, u32[]{:S(2)}, u32[]{:S(2)}) collective-permute-start(f32[1536,16]{0,1:T(8,128)S(1)} %fusion), channel_id=1, source_target_pairs={{0,8},{2,10},{4,12},{6,14},{8,16},{10,18},{12,20},{14,22},{16,24},... | collective-permute-start | bytes 294920
  834.5 18.9 %collective-permute-start.2 = (f32[1536,16]{0,1:T(8,128)S(1)}, f32[1536,16]{0,1:T(8,128)S(1)}, u32[]{:S(2)}, u32[]{:S(2)}) collective-permute-start(f32[1536,16]{0,1:T(8,128)S(1)} %fusion), channel_id=1, source_target_pairs={{0,6},{2,8},{4,10},{6,12},{8,14},{10,16},{12,18},{14,20},{16,22},{... | collective-permute-start | bytes 294920
  839.4 14.0 %collective-permute-start.1 = (f32[1536,16]{0,1:T(8,128)S(1)}, f32[1536,16]{0,1:T(8,128)S(1)}, u32[]{:S(2)}, u32[]{:S(2)}) collective-permute-start(f32[1536,16]{0,1:T(8,128)S(1)} %fusion), channel_id=1, source_target_pairs={{0,4},{2,6},{4,8},{6,10},{8,12},{10,14},{12,16},{14,18},{16,20},{1... | collective-permute-start | bytes 294920
  841.6 11.8 collective-permute-start
  846.6 36.2 %all-to-all-start.11 = ((f32[2,128,768]{2,1,0:T(8,128)}), f32[2,128,768]{2,1,0:T(8,128)S(1)}, u32[]{:S(2)}, u32[]{:S(2)}) async-start(f32[2,128,768]{2,1,0:T(8,128)} %broadcast_in_dim.96), calls=%async_computation.11 | async-start | bytes 1572864 | tf_op jit(solution)/shard_map/all_to_all | solution.py:18
  878.7 274.6 %copy-start.6 = (f32[128,768]{1,0:T(8,128)S(1)}, f32[128,768]{1,0:T(8,128)}, u32[]{:S(2)}) copy-start(f32[128,768]{1,0:T(8,128)} %copy-done.5) | copy-start | bytes 1179652
  878.7 274.6 %copy-start.77 = (f32[128]{0:T(128)S(1)}, f32[128]{0:T(128)}, u32[]{:S(2)}) copy-start(f32[128]{0:T(128)} %get-tuple-element.113) | copy-start | bytes 1540
  (61 other events, 192.6 us)
Sparse Core Ops, SparseCore 0:
  12.5 126.3 all-gather.8
  141.1 195.9 all-gather.4
  434.7 139.9 all-gather.6
  596.7 622.0 all-reduce.8
where the time goes:
time: 1240 us; the launch traced here: 1230 us
  blocking collectives  447 us (36%)
  local copies, waits for them, and re-layouts  280 us (23%)
  waiting for transfers between devices  246 us (20%)
  starting transfers between devices  119 us (10%)
  matrix products  64.8 us (5%)
  other arithmetic  56.8 us (5%)
  between operations  17.2 us (1%)
    unnamed x2, blocking collectives  447 us
    all_gather x2, waiting for transfers between devices, turned_gather(): filled = lax.all_gather(both, axis, axis=0, tiled=True)  138 us
    unnamed x204, local copies, waits for them, and re-layouts  103 us
    all_to_all x9, waiting for transfers between devices, from_everyone(): return lax.all_to_all(copies, axis, split_axis=0, concat_axis=0, tiled=True)  73.5 us
    dot_general x33, matrix products, product(): jnp.einsum(pattern, first_op, second_op, preferred_element_type=jnp.float32)  55.5 us
    unnamed x17, starting transfers between devices  51.3 us
    all_to_all x9, starting transfers between devices, from_everyone(): return lax.all_to_all(copies, axis, split_axis=0, concat_axis=0, tiled=True)  39.6 us
    split x8, local copies, waits for them, and re-layouts, turned_gather(): jnp.split(filled, [sum(widths[:k]) for k in range(1, len(widths))], axis=1)  35.3 us
  transfers between devices with their start and end apart: 33, of which 12 were waited for; matrix products, arithmetic and copies ran while one was open for 44% of the time, Pallas kernels for 0%

commit v1 on v0

v1 whole, which is shorter than its diff:
```python
import jax
import jax.numpy as jnp
from jax import lax
from jax.sharding import Mesh, PartitionSpec as P

HDIM = 64
SLOTS = 8
masked_fill = -1000000000.0
epsilon = 1e-06
ZY = ("z", "y")
EVERY = ("dp", "z", "y", "core")
f32 = jnp.float32
bf16 = jnp.bfloat16


def swap(value, axis):
    return lax.ppermute(value, axis, [(0, 1), (1, 0)])


def ordered(index, own, other, axis):
    first = jnp.where(index == 0, own, other)
    second = jnp.where(index == 0, other, own)
    return jnp.concatenate((first, second), axis=axis)


def mp_sum(partial):
    own = lax.optimization_barrier(partial.astype(bf16))
    return own.astype(f32) + swap(own, "mp").astype(f32)


def dot(a, b):
    return jnp.dot(a, b, preferred_element_type=f32)


def dot_nt(a, b):
    return lax.dot_general(a, b, (((1,), (1,)), ((), ())), preferred_element_type=f32)


def dot_tn(a, b):
    return lax.dot_general(a, b, (((0,), (0,)), ((), ())), preferred_element_type=f32)


def product(pattern, a, b):
    return jnp.einsum(pattern, a, b, preferred_element_type=f32)


def norm_forward(hidden, gain):
    factor = lax.rsqrt(jnp.mean(hidden * hidden, axis=-1, keepdims=True) + epsilon)
    return (hidden * factor * gain).astype(bf16), factor


def norm_backward(hidden, factor, gain, normed_grad):
    scaled = normed_grad * gain
    gain_grad = jnp.sum(normed_grad * hidden * factor, axis=0)
    middle = jnp.mean(hidden * scaled, axis=-1, keepdims=True)
    return factor * scaled - hidden * (factor * factor * factor) * middle, gain_grad


def gelu_parts(gate):
    inside = 0.7978845608028654 * (gate + 0.044715 * gate * gate * gate)
    t = jnp.tanh(inside)
    value = 0.5 * gate * (1.0 + t)
    slope = 0.5 * (1.0 + t) + 0.5 * gate * (1.0 - t * t) * (
        0.7978845608028654 * (1.0 + 3 * 0.044715 * gate * gate)
    )
    return value, slope


def attention_forward(hidden, gain, weights, bias, allowed):
    seq = hidden.shape[0]
    normed, factor = norm_forward(hidden, gain)
    split = []
    for w in weights:
        split.append(dot(normed, w[:, :576]).astype(bf16).reshape(seq, 3, 3, HDIM))
    heads = jnp.concatenate(split, axis=2)
    q, k, v = heads[:, 0], heads[:, 1], heads[:, 2]
    scores = jnp.where(allowed[None], product("qhd,khd->hqk", q, k) * HDIM**-0.5 + bias, masked_fill)
    top = jnp.max(scores, axis=-1, keepdims=True)
    shifted = jnp.exp(scores - top)
    probs = shifted / jnp.sum(shifted, axis=-1, keepdims=True)
    low = probs.astype(bf16)
    mixed = product("hqk,khd->qhd", low, v).astype(bf16)
    parts = [mixed[:, :3].reshape(seq, 192), mixed[:, 3:].reshape(seq, 192)]
    partial = dot_nt(parts[0], weights[0][:, 576:]) + dot_nt(parts[1], weights[1][:, 576:])
    return hidden + mp_sum(partial), (hidden, factor, normed, q, k, v, probs, low, parts)


def attention_backward(upstream, saved, gain, weights, onehot):
    hidden, factor, normed, q, k, v, probs, low, parts = saved
    seq = hidden.shape[0]
    branch = upstream.astype(bf16)
    out_grads = [dot_tn(branch, p) for p in parts]
    mixed_grad = jnp.concatenate(
        [dot(branch, w[:, 576:]).astype(bf16).reshape(seq, 3, HDIM) for w in weights], axis=1
    )
    v_grad = product("hqk,qhd->khd", low, mixed_grad).astype(bf16)
    probs_grad = product("qhd,khd->hqk", mixed_grad, v)
    scores_grad = probs * (probs_grad - jnp.sum(probs * probs_grad, axis=-1, keepdims=True))
    high = scores_grad.astype(bf16)
    rest = (scores_grad - high.astype(f32)).astype(bf16)
    heads = scores_grad.shape[0]
    table_grad = dot(high.reshape(heads, -1), onehot) + dot(rest.reshape(heads, -1), onehot)
    raw = (scores_grad * HDIM**-0.5).astype(bf16)
    q_grad = product("hqk,khd->qhd", raw, k).astype(bf16)
    k_grad = product("hqk,qhd->khd", raw, q).astype(bf16)
    grads = []
    partial = 0.0
    for half in range(2):
        rows = slice(3 * half, 3 * half + 3)
        proj = jnp.stack((q_grad[:, rows], k_grad[:, rows], v_grad[:, rows]), axis=1).reshape(seq, 576)
        grads.append(jnp.concatenate((dot_tn(normed, proj), out_grads[half]), axis=1))
        partial = partial + dot_nt(proj, weights[half][:, :576])
    back, gain_grad = norm_backward(hidden, factor, gain, mp_sum(partial))
    return upstream + back, gain_grad, grads, table_grad


def dense_forward(hidden, gain, weights):
    normed, factor = norm_forward(hidden, gain)
    partial = 0.0
    state = []
    for w in weights:
        gate_up = dot(normed, w[:, :1536])
        value, slope = gelu_parts(gate_up[:, :768])
        up = gate_up[:, 768:]
        inner = (value * up).astype(bf16)
        partial = partial + dot_nt(inner, w[:, 1536:])
        state.append((inner, value, slope * up))
    return hidden + mp_sum(partial), (hidden, factor, normed, state)


def dense_backward(upstream, saved, gain, weights):
    hidden, factor, normed, state = saved
    branch = upstream.astype(bf16)
    grads = []
    partial = 0.0
    for w, (inner, value, slope_up) in zip(weights, state):
        inner_grad = dot(branch, w[:, 1536:])
        both = jnp.concatenate(((inner_grad * slope_up).astype(bf16), (inner_grad * value).astype(bf16)), axis=1)
        grads.append(jnp.concatenate((dot_tn(normed, both), dot_tn(branch, inner)), axis=1))
        partial = partial + dot_nt(both, w[:, :1536])
    back, gain_grad = norm_backward(hidden, factor, gain, mp_sum(partial))
    return upstream + back, gain_grad, grads


def to_own(core, dp, own, other):
    n = own.shape[1]
    both = (own + swap(other.astype(bf16), "core").astype(f32)).astype(bf16)
    both = both.reshape(2, 16, 24, n).transpose(1, 0, 2, 3).reshape(16, 48, n)
    pieces = lax.all_to_all(both, ZY, 0, 0, tiled=True)
    rows = jnp.sum(pieces.astype(f32), axis=0)
    keep = jnp.where(dp == 0, rows[:24], rows[24:])
    send = jnp.where(dp == 0, rows[24:], rows[:24]).astype(bf16)
    rows = keep + swap(send, "dp").astype(f32)
    keep = jnp.where(core == 0, rows[:12], rows[12:])
    send = jnp.where(core == 0, rows[12:], rows[:12])
    return ordered(core, keep[None], swap(send, "core")[None], 0)


def body(
    tokens,
    cotangent,
    routes,
    gate_weights,
    segments,
    buckets,
    norm_gains,
    attention_in,
    attention_out,
    tables,
    dense_in,
    dense_out,
    expert_in,
    expert_out,
):
    core = lax.axis_index("core")
    dp = lax.axis_index("dp")
    seq, width = tokens.shape
    attn = jnp.concatenate(
        (attention_in.transpose(1, 0, 2, 3), attention_out.transpose(2, 0, 1)[:, :, None, :]), axis=2
    )
    attn = attn.reshape(12, 2, 4, 2, 192).transpose(3, 1, 0, 2, 4).reshape(2, 2, 12, 768)
    dense = jnp.concatenate((dense_in, dense_out.T[:, None, :]), axis=1)
    dense = dense.reshape(12, 3, 2, 768).transpose(2, 0, 1, 3).reshape(2, 12, 2304)
    gains = jnp.pad(norm_gains.reshape(4, 12).T, ((0, 0), (0, 124)))
    gains = jnp.broadcast_to(gains[None], (2, 12, 128))
    first = jnp.concatenate((attn[:, 0], gains), axis=2)
    rest = jnp.concatenate((dense, attn[:, 1]), axis=2)

    def spread(halves):
        own = jnp.where(core == 0, halves[0], halves[1])
        send = jnp.where(core == 0, halves[1], halves[0])
        rows = ordered(core, own, swap(send, "core"), 0)
        return ordered(dp, rows, swap(rows, "dp"), 0)

    def natural(filled):
        n = filled.shape[-1]
        return filled.reshape(16, 2, 24, n).transpose(1, 0, 2, 3).reshape(width, n)

    first = spread(first)
    first = lax.all_to_all(jnp.broadcast_to(first[None], (16, *first.shape)), ZY, 0, 0, tiled=True)
    first = natural(first)
    rest = natural(lax.all_gather(spread(rest)[None], ZY, axis=0, tiled=True))
    first_weights = (first[:, :768], swap(first[:, :768], "core"))
    rest_other = swap(rest, "core")
    dense_weights = (rest[:, :2304], rest_other[:, :2304])
    second_weights = (rest[:, 2304:], rest_other[:, 2304:])
    gains = first[:, 768:772].T.astype(f32)

    in_own = expert_in[dp]
    in_other = swap(expert_in[1 - dp], "dp")
    out_own = expert_out[dp]
    out_other = swap(expert_out[1 - dp], "dp")

    positions = jnp.arange(seq, dtype=jnp.int32)
    segment_row = segments[0]
    allowed = (segment_row[:, None] == segment_row[None, :]) & (positions[None, :] <= positions[:, None])
    bucket_ids = jnp.arange(tables.shape[2], dtype=jnp.int32)
    onehot = (buckets.reshape(-1)[:, None] == bucket_ids[None, :]).astype(bf16)
    own_tables = jnp.where(core == 0, tables, jnp.roll(tables, 3, axis=1))
    bias = jnp.einsum(
        "lhb,bx->lhx", own_tables, onehot.astype(f32).T, precision=lax.Precision.HIGHEST
    ).reshape(2, 6, seq, seq)

    experts = 64
    flat = routes.reshape(-1)
    chosen = (flat[:, None] == jnp.arange(experts, dtype=jnp.int32)[None, :]).astype(jnp.int32)
    ranks = jnp.sum((jnp.cumsum(chosen, axis=0) - 1) * chosen, axis=1)
    slots = ((flat % 2) * 32 + flat // 2) * SLOTS + ranks
    slots = slots.reshape(seq, 2)
    hits = slots[None] == jnp.arange(experts * SLOTS, dtype=jnp.int32)[:, None, None]
    fill = jnp.any(hits, axis=2).astype(bf16)
    weighted = jnp.sum(jnp.where(hits, gate_weights[None], 0.0), axis=2)
    slot_weights = jnp.sum(weighted, axis=1, keepdims=True)
    weighted_high = weighted.astype(bf16)
    weighted_rest = (weighted - weighted_high.astype(f32)).astype(bf16)

    def everywhere(rows):
        rows = rows.reshape(experts, SLOTS, width)
        return lax.all_to_all(rows, EVERY, 0, 0, tiled=True).reshape(experts * SLOTS, width)

    dy = everywhere((dot(fill, cotangent) * slot_weights).astype(bf16))

    hidden = tokens.astype(f32)
    hidden, first_state = attention_forward(hidden, gains[0], first_weights, bias[0], allowed)
    hidden, dense_state = dense_forward(hidden, gains[1], dense_weights)
    hidden, second_state = attention_forward(hidden, gains[2], second_weights, bias[1], allowed)

    half = width // 2

    def halves(rows):
        low, high = rows[:, :half], rows[:, half:]
        return jnp.where(dp == 0, low, high), jnp.where(dp == 0, high, low)

    normed, factor = norm_forward(hidden, gains[3])
    rows = everywhere(dot(fill, normed).astype(bf16))
    rows_own, rows_other = halves(rows)
    gate = dot(rows_own, in_own[:, 0]) + dot(rows_other, in_other[:, 0])
    up = dot(rows_own, in_own[:, 1]) + dot(rows_other, in_other[:, 1])
    value, slope = gelu_parts(gate)
    inner = (value * up).astype(bf16)
    y = ordered(dp, dot(inner, out_own).astype(bf16), dot(inner, out_other).astype(bf16), 1)
    y = everywhere(y)
    mixture = dot_tn(weighted_high, y) + dot_tn(weighted_rest, y)
    block_out = (hidden + mp_sum(mixture)).astype(bf16)

    dy_own, dy_other = halves(dy)
    inner_grad = dot_nt(dy_own, out_own) + dot_nt(dy_other, out_other)
    gate_grad = (inner_grad * up * slope).astype(bf16)
    up_grad = (inner_grad * value).astype(bf16)
    rows_grad = ordered(
        dp,
        (dot_nt(gate_grad, in_own[:, 0]) + dot_nt(up_grad, in_own[:, 1])).astype(bf16),
        (dot_nt(gate_grad, in_other[:, 0]) + dot_nt(up_grad, in_other[:, 1])).astype(bf16),
        1,
    )
    normed_grad = mp_sum(dot_tn(fill, everywhere(rows_grad)))
    in_send = jnp.stack((dot_tn(rows_other, gate_grad), dot_tn(rows_other, up_grad)), axis=0).astype(bf16)
    out_send = dot_tn(inner, dy_other).astype(bf16)
    in_keep = jnp.stack((dot_tn(rows_own, gate_grad), dot_tn(rows_own, up_grad)), axis=0)
    out_keep = dot_tn(inner, dy_own)
    in_recv = swap(in_send, "dp")
    out_recv = swap(out_send, "dp")
    expert_in_grad = ordered(dp, in_keep[None], in_recv[None].astype(f32), 0).transpose(0, 2, 1, 3)
    expert_out_grad = ordered(dp, out_keep[None], out_recv[None].astype(f32), 0)

    upstream = cotangent.astype(f32)
    back, gain_moe = norm_backward(hidden, factor, gains[3], normed_grad)
    upstream = upstream + back
    upstream, gain_second, second_grads, table_second = attention_backward(
        upstream, second_state, gains[2], second_weights, onehot
    )
    second_rows = to_own(core, dp, *second_grads)
    upstream, gain_dense, dense_grads = dense_backward(upstream, dense_state, gains[1], dense_weights)
    dense_rows = to_own(core, dp, *dense_grads)
    upstream, gain_first, first_grads, table_first = attention_backward(
        upstream, first_state, gains[0], first_weights, onehot
    )
    gain_columns = jnp.pad(jnp.stack((gain_first, gain_dense, gain_second, gain_moe)).T, ((0, 0), (0, 124)))
    first_grads = [jnp.concatenate((g, gain_columns), axis=1) for g in first_grads]
    first_rows = to_own(core, dp, *first_grads)

    table_grads = jnp.stack((table_first, table_second))
    table_grads = jnp.where(core == 0, table_grads, jnp.roll(table_grads, 3, axis=1))
    copies = jnp.broadcast_to(table_grads.reshape(1, 1, -1), (64, 1, table_grads.size))
    copies = lax.all_to_all(copies, EVERY, 0, 0, tiled=True)
    tables_grad = jnp.sum(copies, axis=0).reshape(table_grads.shape)

    norm_gains_grad = first_rows[0, :, 768:772].T.reshape(2, 2, 12)
    attn_rows = jnp.stack((first_rows[:, :, :768], second_rows)).reshape(2, 2, 12, 4, 192)
    attn_rows = attn_rows.transpose(0, 2, 3, 1, 4).reshape(2, 12, 4, 384)
    attention_in_grad = attn_rows[:, :, :3]
    attention_out_grad = attn_rows[:, :, 3].transpose(0, 2, 1)
    dense_rows = dense_rows.reshape(2, 12, 3, 768).transpose(1, 2, 0, 3).reshape(12, 3, 1536)
    dense_in_grad = dense_rows[:, :2]
    dense_out_grad = dense_rows[:, 2].T
    return (
        block_out,
        upstream.astype(bf16),
        norm_gains_grad,
        attention_in_grad,
        attention_out_grad,
        tables_grad,
        dense_in_grad,
        dense_out_grad,
        expert_in_grad,
        expert_out_grad,
    )


def solution(mesh):
    fine = Mesh(mesh.devices.reshape(2, 4, 4, 2, 2), ("dp", "z", "y", "core", "mp"))
    expert = ("z", "y", "core")
    rows = P(EVERY, None)
    weights = (
        P(None, None, EVERY),
        P(None, EVERY, None, "mp"),
        P(None, "mp", EVERY),
        P(None, "mp", None),
        P(EVERY, None, "mp"),
        P("mp", EVERY),
        P(expert, "dp", None, "mp"),
        P(expert, "mp", "dp"),
    )
    return jax.shard_map(
        body,
        mesh=fine,
        in_specs=(rows, rows, rows, rows, rows, P(), *weights),
        out_specs=(rows, rows, *weights),
        check_vma=False,
    )
```

time: 1240 us -> 601 us (0.48)
  blocking collectives: 447 us -> 0 us
  local copies, waits for them, and re-layouts: 280 us -> 83.8 us
  matrix products: 64.8 us -> 114 us
  waiting for transfers between devices: 246 us -> 212 us
    unnamed x2 -> x0, blocking collectives: 447 us -> none
    all_gather x3 -> x1, waiting for transfers between devices: 138 us -> 50.6 us  [body(): rest = natural(lax.all_gather(spread(rest)[None], ZY, axis=0, tiled=True))]
    ppermute x0 -> x27, waiting for transfers between devices: none -> 73.4 us  [swap(): return lax.ppermute(value, axis, [(0, 1), (1, 0)])]
    unnamed x204 -> x233, local copies, waits for them, and re-layouts: 103 us -> 33.5 us
    unnamed x17 -> x0, starting transfers between devices: 51.3 us -> none
    dot_general x40 -> x76, matrix products: 64.8 us -> 114 us  [the longest x24 37.9 us: dot(): return jnp.dot(a, b, preferred_element_type=f32)]
    split x12 -> x0, local copies, waits for them, and re-layouts: 47.6 us -> none  [the longest x8 35.3 us: turned_gather(): jnp.split(filled, [sum(widths[:k]) for k in range(1, len(widths))], axis=1)]
    ppermute x0 -> x27, starting transfers between devices: none -> 46.2 us  [swap(): return lax.ppermute(value, axis, [(0, 1), (1, 0)])]
  transfers between devices with their start and end apart: 33 -> 37, of which waited for: 12 -> 21; matrix products, arithmetic and copies ran while one was open for 44% -> 36% of each run, Pallas kernels for 0% -> 0%
where the time goes in v1:
time: 601 us; the launch traced here: 590 us
  waiting for transfers between devices  212 us (35%)
  matrix products  114 us (19%)
  starting transfers between devices  107 us (18%)
  local copies, waits for them, and re-layouts  83.8 us (14%)
  other arithmetic  57.4 us (10%)
  between operations  16.4 us (3%)
    ppermute x27, waiting for transfers between devices, swap(): return lax.ppermute(value, axis, [(0, 1), (1, 0)])  73.4 us
    all_to_all x4, waiting for transfers between devices, everywhere(): lax.all_to_all(rows, EVERY, 0, 0, tiled=True)  59.9 us
    all_gather x1, waiting for transfers between devices, body(): rest = natural(lax.all_gather(spread(rest)[None], ZY, axis=0, tiled=True))  50.6 us
    ppermute x27, starting transfers between devices, swap(): return lax.ppermute(value, axis, [(0, 1), (1, 0)])  46.2 us
    dot_general x24, matrix products, dot(): return jnp.dot(a, b, preferred_element_type=f32)  37.9 us
    dot_general x18, matrix products, dot_nt(): lax.dot_general(a, b, (((1,), (1,)), ((), ())), preferred_element_type=f32)  34.3 us
    unnamed x233, local copies, waits for them, and re-layouts  33.5 us
    dot_general x21, matrix products, dot_tn(): lax.dot_general(a, b, (((0,), (0,)), ((), ())), preferred_element_type=f32)  30.9 us
  transfers between devices with their start and end apart: 37, of which 21 were waited for; matrix products, arithmetic and copies ran while one was open for 36% of the time, Pallas kernels for 0%

profile of v1, /device:TPU:1, one launch (start us, length us, event | category | flops | bytes accessed | tf_op | source)
XLA Modules:
  0.0 589.7 jit_solution(1667205181629455563)
XLA Ops:
  16.2 3.8 collective-permute-done.5
  27.5 7.9 %all-to-all-start = ((bf16[16,48,896]{2,1,0:T(8,128)(2,1)}), bf16[16,48,896]{2,1,0:T(8,128)(2,1)}, u32[]{:S(2)}, u32[]{:S(2)}) async-start(bf16[16,48,896]{2,1,0:T(8,128)(2,1)} %broadcast_in_dim.37), calls=%async_computation | async-start | bytes 2752512 | tf_op jit(solution)/shard_map/all_to_all | solution.py:200
  38.3 50.6 %all-gather.3.cloned.1.call-done = bf16[768,3072]{1,0:T(8,128)(2,1)} async-done(((bf16[48,3072]{1,0:T(8,128)(2,1)}), bf16[768,3072]{1,0:T(8,128)(2,1)}) %all-gather.3.cloned.1.call-update) | async-done | bytes 4718608 | tf_op jit(solution)/shard_map/all_gather | solution.py:202
  88.9 4.9 copy.502
  100.7 3.0 collective-permute-done.2
  109.4 2.1 fusion.61
  111.5 2.7 collective-permute-start.3
  114.9 2.2 fusion.36
  117.1 7.0 %all-to-all-start.3 = ((bf16[64,8,768]{2,1,0:T(8,128)(2,1)}), bf16[64,8,768]{2,1,0:T(8,128)(2,1)}, u32[]{:S(2)}, u32[]{:S(2)}) async-start(bf16[64,8,768]{2,1,0:T(8,128)(2,1)} %fusion.36), calls=%async_computation.3 | async-start | bytes 1572864 | tf_op jit(solution)/shard_map/all_to_all | solution.py:239
  125.8 2.1 fusion.34
  130.1 2.1 fusion.30
  157.3 2.4 collective-permute-start.8
  159.8 5.6 constant_dynamic-slice_fusion
  169.1 3.5 collective-permute-done.8
  174.8 11.2 %all-to-all-start.1 = ((bf16[64,8,768]{2,1,0:T(8,128)(2,1)}), bf16[64,8,768]{2,1,0:T(8,128)(2,1)}, u32[]{:S(2)}, u32[]{:S(2)}) async-start(bf16[64,8,768]{2,1,0:T(8,128)(2,1)} %fusion.37), calls=%async_computation.1 | async-start | bytes 1572864 | tf_op jit(solution)/shard_map/all_to_all | solution.py:239
  192.0 2.1 fusion.55
  194.1 4.0 convolution_add_fusion
  198.1 37.7 %all-to-all-done.1 = bf16[64,8,768]{2,1,0:T(8,128)(2,1)} async-done(((bf16[64,8,768]{2,1,0:T(8,128)(2,1)}), bf16[64,8,768]{2,1,0:T(8,128)(2,1)}, u32[]{:S(2)}, u32[]{:S(2)}) %all-to-all-start.1) | async-done | bytes 786464 | tf_op jit(solution)/shard_map/all_to_all | solution.py:239
  242.9 2.6 fusion.86
  246.5 2.4 convolution_add_fusion.1
  249.0 5.9 fusion.14
  256.0 2.1 broadcast_select_fusion.5
  259.1 2.3 copy.513
  261.4 2.3 fusion.84
  264.6 2.2 fusion.87
  266.8 2.1 broadcast_select_fusion.1
  270.1 5.1 all-to-all-start.4
  275.3 3.7 convolution_convert_fusion.1
  284.1 5.7 all-to-all-done.4
  289.8 4.9 all-to-all-start.2
  294.7 3.4 pad_maximum_fusion.3
  299.6 2.2 convolution_bitcast_fusion.1
  301.8 2.2 convolution_bitcast_fusion
  306.9 16.5 %all-to-all-done.2 = bf16[64,8,768]{2,1,0:T(8,128)(2,1)S(1)} async-done(((bf16[64,8,768]{2,1,0:T(8,128)(2,1)}), bf16[64,8,768]{2,1,0:T(8,128)(2,1)S(1)}, u32[]{:S(2)}, u32[]{:S(2)}) %all-to-all-start.2) | async-done | bytes 786464 | tf_op jit(solution)/shard_map/all_to_all | solution.py:239
  324.1 2.1 collective-permute-start.11
  326.2 48.6 %collective-permute-done.12 = bf16[128,768]{1,0:T(8,128)(2,1)} collective-permute-done((bf16[128,768]{1,0:T(8,128)(2,1)}, bf16[128,768]{1,0:T(8,128)(2,1)}, u32[]{:S(2)}, u32[]{:S(2)}) %collective-permute-start.12) | collective-permute-done | bytes 196640 | tf_op jit(solution)/shard_map/ppermute | solution.py:17
  376.0 2.9 collective-permute-done.11
  406.2 2.6 fusion.32
  411.4 2.6 fusion.64
  422.0 3.0 fusion.164
  425.0 4.5 fusion.18
  437.8 2.1 convolution_convert_fusion.6
  440.5 2.1 collective-permute-start.15
  443.4 5.3 collective-permute-done.15
  452.2 8.6 %all-to-all-start.7 = ((f32[64,1,384]{2,1,0:T(1,128)}), f32[64,1,384]{2,1,0:T(1,128)S(1)}, u32[]{:S(2)}, u32[]{:S(2)}) async-start(f32[64,1,384]{2,1,0:T(1,128)} %broadcast_in_dim.43), calls=%async_computation.7 | async-start | bytes 196608 | tf_op jit(solution)/shard_map/all_to_all | solution.py:305
  460.9 2.5 fusion.20
  463.4 2.4 copy.527
  465.8 2.5 copy.528
  469.1 6.0 %all-to-all-start.6 = ((bf16[16,48,768]{2,1,0:T(8,128)(2,1)}), bf16[16,48,768]{2,1,0:T(8,128)(2,1)}, u32[]{:S(2)}, u32[]{:S(2)}) async-start(bf16[16,48,768]{2,1,0:T(8,128)(2,1)} %bitcast.372), calls=%async_computation.6 | async-start | bytes 2359296 | tf_op jit(solution)/shard_map/all_to_all | solution.py:149
  475.1 4.2 pad_maximum_fusion.1
  480.8 2.7 fusion.15
  486.6 6.5 %all-to-all-done.6 = bf16[16,48,768]{2,1,0:T(8,128)(2,1)} async-done(((bf16[16,48,768]{2,1,0:T(8,128)(2,1)}), bf16[16,48,768]{2,1,0:T(8,128)(2,1)}, u32[]{:S(2)}, u32[]{:S(2)}) %all-to-all-start.6) | async-done | bytes 1179680 | tf_op jit(solution)/shard_map/all_to_all | solution.py:149
  493.1 4.8 all-to-all-start.5
  498.9 3.8 fusion.4
  504.7 11.9 %all-to-all-done.5 = bf16[16,48,896]{2,1,0:T(8,128)(2,1)} async-done(((bf16[16,48,896]{2,1,0:T(8,128)(2,1)}), bf16[16,48,896]{2,1,0:T(8,128)(2,1)}, u32[]{:S(2)}, u32[]{:S(2)}) %all-to-all-start.5) | async-done | bytes 1376288 | tf_op jit(solution)/shard_map/all_to_all | solution.py:149
  516.6 5.0 all-to-all-start.8
  521.6 5.3 fusion.5
  529.8 3.2 maximum_bitcast_fusion
  533.0 14.6 %copy.545 = f32[2,384,2,1536]{3,2,1,0:T(2,128)} copy(f32[2,384,2,1536]{3,1,2,0:T(8,128)S(1)} %maximum_bitcast_fusion) | data formatting | bytes 18874368
  549.3 4.0 collective-permute-start.21
  553.3 3.7 collective-permute-start.18
  557.9 8.6 %all-to-all-done.8 = bf16[16,48,2304]{2,1,0:T(8,128)(2,1)} async-done(((bf16[16,48,2304]{2,1,0:T(8,128)(2,1)}), bf16[16,48,2304]{2,1,0:T(8,128)(2,1)}, u32[]{:S(2)}, u32[]{:S(2)}) %all-to-all-start.8) | async-done | bytes 3538976 | tf_op jit(solution)/shard_map/all_to_all | solution.py:149
  566.5 2.6 convert_reduce_fusion
  572.9 5.8 collective-permute-start.24
  (484 shorter events, 168.4 us)
Async XLA Ops:
  7.2 129.9 %copy-start = (bf16[2,1536,384]{2,1,0:T(8,128)(2,1)S(1)}, bf16[2,1536,384]{2,1,0:T(8,128)(2,1)}, u32[]{:S(2)}) copy-start(bf16[2,1536,384]{2,1,0:T(8,128)(2,1)} %param.27) | copy-start | bytes 7077892
  7.2 81.7 %all-gather.3.cloned.1.call-start = ((), (), s32[]{:S(2)}) async-start(), calls=%async_computation.9 | async-start | bytes 5013504 | tf_op jit(solution)/shard_map/all_gather | solution.py:202
  9.5 11.3 %copy-start.96 = (bf16[2,2,12]{2,1,0:T(2,128)(2,1)S(1)}, bf16[2,2,12]{2,1,0:T(2,128)(2,1)}, u32[]{:S(2)}) copy-start(bf16[2,2,12]{2,1,0:T(2,128)(2,1)} %param.20) | copy-start | bytes 292
  11.4 13.2 %copy-start.82 = (f32[2,6,32]{2,0,1:T(2,128)S(1)}, f32[2,6,32]{2,0,1:T(2,128)}, u32[]{:S(2)}) copy-start(f32[2,6,32]{2,0,1:T(2,128)} %param.23) | copy-start | bytes 4612
  11.4 13.2 %copy-start.93 = (s32[128,2]{0,1:T(2,128)S(1)}, s32[128,2]{0,1:T(2,128)}, u32[]{:S(2)}) copy-start(s32[128,2]{0,1:T(2,128)} %param.16) | copy-start | bytes 3076
  12.3 2.4 collective-permute-start.4
  14.9 5.2 collective-permute-start.5
  21.1 2.1 collective-permute-start
  23.3 3.0 collective-permute-start.1
  26.3 10.3 %copy-start.78 = (s32[128,128]{1,0:T(8,128)S(1)}, s32[128,128]{1,0:T(8,128)}, u32[]{:S(2)}) copy-start(s32[128,128]{1,0:T(8,128)} %param.19) | copy-start | bytes 196612
  27.5 68.8 %all-to-all-start = ((bf16[16,48,896]{2,1,0:T(8,128)(2,1)}), bf16[16,48,896]{2,1,0:T(8,128)(2,1)}, u32[]{:S(2)}, u32[]{:S(2)}) async-start(bf16[16,48,896]{2,1,0:T(8,128)(2,1)} %broadcast_in_dim.37), calls=%async_computation | async-start | bytes 2752512 | tf_op jit(solution)/shard_map/all_to_all | solution.py:200
  93.8 36.3 %collective-permute-start.6 = (bf16[768,3072]{1,0:T(8,128)(2,1)}, bf16[768,3072]{1,0:T(8,128)(2,1)}, u32[]{:S(2)}, u32[]{:S(2)}) collective-permute-start(bf16[768,3072]{1,0:T(8,128)(2,1)} %bitcast.27), channel_id=1, source_target_pairs={{0,2},{2,0},{1,3},{3,1},{4,6},{6,4},{5,7},{7,5},{8,10},{10,8},{9,1... | collective-permute-start | bytes 14155784 | tf_op jit(solution)/shard_map/ppermute | solution.py:17
  97.8 5.9 collective-permute-start.2
  100.7 25.0 %copy-start.45 = (bf16[128,576]{0,1:T(8,128)(2,1)}, bf16[128,576]{0,1:T(8,128)(2,1)S(1)}, u32[]{:S(2)}) copy-start(bf16[128,576]{0,1:T(8,128)(2,1)S(1)} %convolution_convert_fusion.16) | copy-start | bytes 442372
  106.9 10.3 %copy-start.91 = (f32[6,128]{1,0:T(8,128)}, f32[6,128]{1,0:T(8,128)S(1)}, u32[]{:S(2)}) copy-start(f32[6,128]{1,0:T(8,128)S(1)} %get-tuple-element.204) | copy-start | bytes 9220
  111.5 14.2 %copy-start.74 = (f32[768]{0:T(1024)S(1)}, f32[768]{0:T(1024)}, u32[]{:S(2)}) copy-start(f32[768]{0:T(1024)} %get-tuple-element.110) | copy-start | bytes 9220
  111.5 12.6 %collective-permute-start.3 = (bf16[128,768]{1,0:T(8,128)(2,1)}, bf16[128,768]{1,0:T(8,128)(2,1)S(1)}, u32[]{:S(2)}, u32[]{:S(2)}) collective-permute-start(bf16[128,768]{1,0:T(8,128)(2,1)} %fusion.61), channel_id=1, source_target_pairs={{0,1},{1,0},{2,3},{3,2},{4,5},{5,4},{6,7},{7,6},{8,9},{9,8},{10,11... | collective-permute-start | bytes 589832 | tf_op jit(solution)/shard_map/ppermute | solution.py:17
  117.1 57.7 %all-to-all-start.3 = ((bf16[64,8,768]{2,1,0:T(8,128)(2,1)}), bf16[64,8,768]{2,1,0:T(8,128)(2,1)}, u32[]{:S(2)}, u32[]{:S(2)}) async-start(bf16[64,8,768]{2,1,0:T(8,128)(2,1)} %fusion.36), calls=%async_computation.3 | async-start | bytes 1572864 | tf_op jit(solution)/shard_map/all_to_all | solution.py:239
  135.2 7.7 %copy-start.57 = (bf16[128,768]{1,0:T(8,128)(2,1)}, bf16[128,768]{1,0:T(8,128)(2,1)S(1)}, u32[]{:S(2)}) copy-start(bf16[128,768]{1,0:T(8,128)(2,1)S(1)} %fusion.62) | copy-start | bytes 589828
  135.2 7.8 %collective-permute-start.7 = (bf16[128,768]{1,0:T(8,128)(2,1)S(1)}, bf16[128,768]{1,0:T(8,128)(2,1)}, u32[]{:S(2)}, u32[]{:S(2)}) collective-permute-start(bf16[128,768]{1,0:T(8,128)(2,1)S(1)} %fusion.62), channel_id=1, source_target_pairs={{0,1},{1,0},{2,3},{3,2},{4,5},{5,4},{6,7},{7,6},{8,9},{9,8},{10,11... | collective-permute-start | bytes 589832 | tf_op jit(solution)/shard_map/ppermute | solution.py:17
  138.2 55.8 %collective-permute-start.10 = (bf16[1536,384]{1,0:T(8,128)(2,1)}, bf16[1536,384]{1,0:T(8,128)(2,1)}, u32[]{:S(2)}, u32[]{:S(2)}) collective-permute-start(bf16[1536,384]{1,0:T(8,128)(2,1)} %dynamic-slice_bitcast_fusion), channel_id=1, source_target_pairs={{0,64},{64,0},{1,65},{65,1},{2,66},{66,2},{3,67},{67,3},{4,68},{68... | collective-permute-start | bytes 3538952 | tf_op jit(solution)/shard_map/ppermute | solution.py:17
  154.5 10.9 %copy-start.60 = (bf16[128,3,64]{0,2,1:T(8,128)(2,1)}, bf16[128,3,64]{0,2,1:T(8,128)(2,1)S(1)}, u32[]{:S(2)}) copy-start(bf16[128,3,64]{0,2,1:T(8,128)(2,1)S(1)} %get-tuple-element.180) | copy-start | bytes 147460
  154.5 10.9 %copy-start.64 = (bf16[128,3,64]{0,2,1:T(8,128)(2,1)}, bf16[128,3,64]{0,2,1:T(8,128)(2,1)S(1)}, u32[]{:S(2)}) copy-start(bf16[128,3,64]{0,2,1:T(8,128)(2,1)S(1)} %get-tuple-element.181) | copy-start | bytes 147460
  157.3 15.2 %collective-permute-start.8 = (bf16[128,768]{1,0:T(8,128)(2,1)S(1)}, bf16[128,768]{1,0:T(8,128)(2,1)S(1)}, u32[]{:S(2)}, u32[]{:S(2)}) collective-permute-start(bf16[128,768]{1,0:T(8,128)(2,1)S(1)} %fusion.63), channel_id=1, source_target_pairs={{0,1},{1,0},{2,3},{3,2},{4,5},{5,4},{6,7},{7,6},{8,9},{9,8},{10,11... | collective-permute-start | bytes 589832 | tf_op jit(solution)/shard_map/ppermute | solution.py:17
  167.1 79.4 %collective-permute-start.9 = (bf16[384,2,1536]{2,0,1:T(8,128)(2,1)}, bf16[384,2,1536]{2,0,1:T(8,128)(2,1)}, u32[]{:S(2)}, u32[]{:S(2)}) collective-permute-start(bf16[384,2,1536]{2,0,1:T(8,128)(2,1)} %bitcast.349), channel_id=1, source_target_pairs={{0,64},{64,0},{1,65},{65,1},{2,66},{66,2},{3,67},{67,3},{4,68},{68... | collective-permute-start | bytes 7077896 | tf_op jit(solution)/shard_map/ppermute | solution.py:17
  174.8 61.0 %all-to-all-start.1 = ((bf16[64,8,768]{2,1,0:T(8,128)(2,1)}), bf16[64,8,768]{2,1,0:T(8,128)(2,1)}, u32[]{:S(2)}, u32[]{:S(2)}) async-start(bf16[64,8,768]{2,1,0:T(8,128)(2,1)} %fusion.37), calls=%async_computation.1 | async-start | bytes 1572864 | tf_op jit(solution)/shard_map/all_to_all | solution.py:239
  270.1 19.6 %all-to-all-start.4 = ((bf16[64,8,768]{2,1,0:T(8,128)(2,1)}), bf16[64,8,768]{2,1,0:T(8,128)(2,1)S(1)}, u32[]{:S(2)}, u32[]{:S(2)}) async-start(bf16[64,8,768]{2,1,0:T(8,128)(2,1)} %bitcast.374), calls=%async_computation.4 | async-start | bytes 1572864 | tf_op jit(solution)/shard_map/all_to_all | solution.py:239
  279.0 146.0 %collective-permute-start.26 = (bf16[1536,384]{1,0:T(8,128)(2,1)}, bf16[1536,384]{1,0:T(8,128)(2,1)}, u32[]{:S(2)}, u32[]{:S(2)}) collective-permute-start(bf16[1536,384]{1,0:T(8,128)(2,1)} %convolution_convert_fusion.1), channel_id=1, source_target_pairs={{0,64},{64,0},{1,65},{65,1},{2,66},{66,2},{3,67},{67,3},{4,68},{68... | collective-permute-start | bytes 3538952 | tf_op jit(solution)/shard_map/ppermute | solution.py:17
  289.8 33.7 %all-to-all-start.2 = ((bf16[64,8,768]{2,1,0:T(8,128)(2,1)}), bf16[64,8,768]{2,1,0:T(8,128)(2,1)S(1)}, u32[]{:S(2)}, u32[]{:S(2)}) async-start(bf16[64,8,768]{2,1,0:T(8,128)(2,1)} %bitcast.48), calls=%async_computation.2 | async-start | bytes 1572864 | tf_op jit(solution)/shard_map/all_to_all | solution.py:239
  298.1 223.5 %collective-permute-start.25 = (bf16[2,384,1536]{2,1,0:T(8,128)(2,1)}, bf16[2,384,1536]{2,1,0:T(8,128)(2,1)}, u32[]{:S(2)}, u32[]{:S(2)}) collective-permute-start(bf16[2,384,1536]{2,1,0:T(8,128)(2,1)} %pad_maximum_fusion.3), channel_id=1, source_target_pairs={{0,64},{64,0},{1,65},{65,1},{2,66},{66,2},{3,67},{67,3},{4,68},{68... | collective-permute-start | bytes 7077896 | tf_op jit(solution)/shard_map/ppermute | solution.py:17
  301.8 21.7 %copy-start.29 = (f32[512,128]{1,0:T(8,128)S(1)}, f32[512,128]{1,0:T(8,128)}, u32[]{:S(2)}) copy-start(f32[512,128]{1,0:T(8,128)} %get-tuple-element.113) | copy-start | bytes 786436
  303.9 70.9 %copy-start.19 = (f32[128,768]{1,0:T(8,128)S(1)}, f32[128,768]{1,0:T(8,128)}, u32[]{:S(2)}) copy-start(f32[128,768]{1,0:T(8,128)} %copy-done.18) | copy-start | bytes 1179652
  303.9 75.0 %copy-start.100 = (f32[128]{0:T(128)S(1)}, f32[128]{0:T(128)}, u32[]{:S(2)}) copy-start(f32[128]{0:T(128)} %get-tuple-element.202) | copy-start | bytes 1540
  304.9 74.0 %copy-start.56 = (bf16[128,768]{1,0:T(8,128)(2,1)S(1)}, bf16[128,768]{1,0:T(8,128)(2,1)}, u32[]{:S(2)}) copy-start(bf16[128,768]{1,0:T(8,128)(2,1)} %param.15) | copy-start | bytes 589828
  304.9 69.9 %collective-permute-start.12 = (bf16[128,768]{1,0:T(8,128)(2,1)}, bf16[128,768]{1,0:T(8,128)(2,1)}, u32[]{:S(2)}, u32[]{:S(2)}) collective-permute-start(bf16[128,768]{1,0:T(8,128)(2,1)} %convolution_convert_fusion.12), channel_id=1, source_target_pairs={{0,1},{1,0},{2,3},{3,2},{4,5},{5,4},{6,7},{7,6},{8,9},{9,8},{10,11... | collective-permute-start | bytes 589832 | tf_op jit(solution)/shard_map/ppermute | solution.py:17
  323.8 58.6 %copy-start.61 = (bf16[128,3,64]{0,2,1:T(8,128)(2,1)S(1)}, bf16[128,3,64]{0,2,1:T(8,128)(2,1)}, u32[]{:S(2)}) copy-start(bf16[128,3,64]{0,2,1:T(8,128)(2,1)} %copy-done.60) | copy-start | bytes 147460
  324.1 54.8 %collective-permute-start.11 = (bf16[128,768]{1,0:T(8,128)(2,1)S(1)}, bf16[128,768]{1,0:T(8,128)(2,1)S(1)}, u32[]{:S(2)}, u32[]{:S(2)}) collective-permute-start(bf16[128,768]{1,0:T(8,128)(2,1)S(1)} %fusion.58), channel_id=1, source_target_pairs={{0,1},{1,0},{2,3},{3,2},{4,5},{5,4},{6,7},{7,6},{8,9},{9,8},{10,11... | collective-permute-start | bytes 589832 | tf_op jit(solution)/shard_map/ppermute | solution.py:17
  396.9 7.2 %collective-permute-start.13 = (bf16[128,768]{1,0:T(8,128)(2,1)S(1)}, bf16[128,768]{1,0:T(8,128)(2,1)S(1)}, u32[]{:S(2)}, u32[]{:S(2)}) collective-permute-start(bf16[128,768]{1,0:T(8,128)(2,1)S(1)} %fusion.59), channel_id=1, source_target_pairs={{0,1},{1,0},{2,3},{3,2},{4,5},{5,4},{6,7},{7,6},{8,9},{9,8},{10,11... | collective-permute-start | bytes 589832 | tf_op jit(solution)/shard_map/ppermute | solution.py:17
  400.0 60.9 %collective-permute-start.19 = (bf16[768,768]{0,1:T(8,128)(2,1)}, bf16[768,768]{0,1:T(8,128)(2,1)}, u32[]{:S(2)}, u32[]{:S(2)}) collective-permute-start(bf16[768,768]{0,1:T(8,128)(2,1)} %pad_maximum_fusion.5), channel_id=1, source_target_pairs={{0,2},{2,0},{1,3},{3,1},{4,6},{6,4},{5,7},{7,5},{8,10},{10,8},{9,1... | collective-permute-start | bytes 3538952 | tf_op jit(solution)/shard_map/ppermute | solution.py:17
  415.1 14.5 %collective-permute-start.14 = (bf16[128,768]{1,0:T(8,128)(2,1)S(1)}, bf16[128,768]{1,0:T(8,128)(2,1)S(1)}, u32[]{:S(2)}, u32[]{:S(2)}) collective-permute-start(bf16[128,768]{1,0:T(8,128)(2,1)S(1)} %fusion.64), channel_id=1, source_target_pairs={{0,1},{1,0},{2,3},{3,2},{4,5},{5,4},{6,7},{7,6},{8,9},{9,8},{10,11... | collective-permute-start | bytes 589832 | tf_op jit(solution)/shard_map/ppermute | solution.py:17
  418.0 80.8 %collective-permute-start.22 = (bf16[768,2304]{1,0:T(8,128)(2,1)}, bf16[768,2304]{1,0:T(8,128)(2,1)}, u32[]{:S(2)}, u32[]{:S(2)}) collective-permute-start(bf16[768,2304]{1,0:T(8,128)(2,1)} %pad_maximum_fusion.2), channel_id=1, source_target_pairs={{0,2},{2,0},{1,3},{3,1},{4,6},{6,4},{5,7},{7,5},{8,10},{10,8},{9,1... | collective-permute-start | bytes 10616840 | tf_op jit(solution)/shard_map/ppermute | solution.py:17
  437.7 10.9 %copy-start.85 = (f32[128]{0:T(128)S(1)}, f32[128]{0:T(128)}, u32[]{:S(2)}) copy-start(f32[128]{0:T(128)} %copy-done.84) | copy-start | bytes 1540
  437.8 11.6 %copy-start.83 = (f32[1,768]{1,0:T(1,128)S(1)}, f32[1,768]{1,0:T(1,128)}, u32[]{:S(2)}) copy-start(f32[1,768]{1,0:T(1,128)} %stack.118) | copy-start | bytes 9220
  440.5 8.9 %copy-start.20 = (bf16[768,576]{0,1:T(8,128)(2,1)S(1)}, bf16[768,576]{0,1:T(8,128)(2,1)}, u32[]{:S(2)}) copy-start(bf16[768,576]{0,1:T(8,128)(2,1)} %convolution_convert_fusion.6) | copy-start | bytes 2654212
  440.5 8.1 %collective-permute-start.15 = (bf16[128,768]{1,0:T(8,128)(2,1)S(1)}, bf16[128,768]{1,0:T(8,128)(2,1)S(1)}, u32[]{:S(2)}, u32[]{:S(2)}) collective-permute-start(bf16[128,768]{1,0:T(8,128)(2,1)S(1)} %fusion.60), channel_id=1, source_target_pairs={{0,1},{1,0},{2,3},{3,2},{4,5},{5,4},{6,7},{7,6},{8,9},{9,8},{10,11... | collective-permute-start | bytes 589832 | tf_op jit(solution)/shard_map/ppermute | solution.py:17
  443.1 17.8 %copy-start.8 = (f32[768,576]{0,1:T(8,128)S(1)}, f32[768,576]{0,1:T(8,128)}, u32[]{:S(2)}) copy-start(f32[768,576]{0,1:T(8,128)} %fusion.264) | copy-start | bytes 5308420
  443.1 17.8 %copy-start.28 = (f32[768,192]{0,1:T(8,128)S(1)}, f32[768,192]{0,1:T(8,128)}, u32[]{:S(2)}) copy-start(f32[768,192]{0,1:T(8,128)} %fusion.265) | copy-start | bytes 1769476
  450.6 30.1 %collective-permute-start.16 = (bf16[768,896]{0,1:T(8,128)(2,1)}, bf16[768,896]{0,1:T(8,128)(2,1)}, u32[]{:S(2)}, u32[]{:S(2)}) collective-permute-start(bf16[768,896]{0,1:T(8,128)(2,1)} %pad_maximum_fusion.4), channel_id=1, source_target_pairs={{0,2},{2,0},{1,3},{3,1},{4,6},{6,4},{5,7},{7,5},{8,10},{10,8},{9,1... | collective-permute-start | bytes 4128776 | tf_op jit(solution)/shard_map/ppermute | solution.py:17
  452.2 16.9 %all-to-all-start.7 = ((f32[64,1,384]{2,1,0:T(1,128)}), f32[64,1,384]{2,1,0:T(1,128)S(1)}, u32[]{:S(2)}, u32[]{:S(2)}) async-start(f32[64,1,384]{2,1,0:T(1,128)} %broadcast_in_dim.43), calls=%async_computation.7 | async-start | bytes 196608 | tf_op jit(solution)/shard_map/all_to_all | solution.py:305
  465.8 9.3 %copy-start.7 = (f32[1,1536,384]{2,1,0:T(8,128)S(1)}, f32[1,1536,384]{2,1,0:T(8,128)}, u32[]{:S(2)}) copy-start(f32[1,1536,384]{2,1,0:T(8,128)} %get-tuple-element.139) | copy-start | bytes 7077892
  469.1 24.0 %all-to-all-start.6 = ((bf16[16,48,768]{2,1,0:T(8,128)(2,1)}), bf16[16,48,768]{2,1,0:T(8,128)(2,1)}, u32[]{:S(2)}, u32[]{:S(2)}) async-start(bf16[16,48,768]{2,1,0:T(8,128)(2,1)} %bitcast.372), calls=%async_computation.6 | async-start | bytes 2359296 | tf_op jit(solution)/shard_map/all_to_all | solution.py:149
  485.3 12.6 %copy-start.101 = (f32[128]{0:T(128)S(1)}, f32[128]{0:T(128)}, u32[]{:S(2)}) copy-start(f32[128]{0:T(128)} %get-tuple-element.107) | copy-start | bytes 1540
  485.3 12.6 %copy-start.38 = (f32[128,768]{1,0:T(8,128)S(1)}, f32[128,768]{1,0:T(8,128)}, u32[]{:S(2)}) copy-start(f32[128,768]{1,0:T(8,128)} %get-tuple-element.119) | copy-start | bytes 1179652
  485.3 12.6 %copy-start.86 = (f32[128]{0:T(128)S(1)}, f32[128]{0:T(128)}, u32[]{:S(2)}) copy-start(f32[128]{0:T(128)} %copy-done.84) | copy-start | bytes 1540
  485.3 12.6 %copy-start.97 = (f32[128]{0:T(128)S(1)}, f32[128]{0:T(128)}, u32[]{:S(2)}) copy-start(f32[128]{0:T(128)} %get-tuple-element.196) | copy-start | bytes 1540
  486.6 12.3 %copy-start.4 = (f32[768,768]{1,0:T(8,128)S(1)}, f32[768,768]{1,0:T(8,128)}, u32[]{:S(2)}) copy-start(f32[768,768]{1,0:T(8,128)} %fusion.262) | copy-start | bytes 7077892
  493.1 23.5 %all-to-all-start.5 = ((bf16[16,48,896]{2,1,0:T(8,128)(2,1)}), bf16[16,48,896]{2,1,0:T(8,128)(2,1)}, u32[]{:S(2)}, u32[]{:S(2)}) async-start(bf16[16,48,896]{2,1,0:T(8,128)(2,1)} %bitcast.369), calls=%async_computation.5 | async-start | bytes 2752512 | tf_op jit(solution)/shard_map/all_to_all | solution.py:149
  516.6 49.9 %all-to-all-start.8 = ((bf16[16,48,2304]{2,1,0:T(8,128)(2,1)}), bf16[16,48,2304]{2,1,0:T(8,128)(2,1)}, u32[]{:S(2)}, u32[]{:S(2)}) async-start(bf16[16,48,2304]{2,1,0:T(8,128)(2,1)} %bitcast.364), calls=%async_computation.8 | async-start | bytes 7077888 | tf_op jit(solution)/shard_map/all_to_all | solution.py:149
  528.3 19.2 %collective-permute-start.20 = (bf16[24,768]{1,0:T(8,128)(2,1)S(1)}, bf16[24,768]{1,0:T(8,128)(2,1)S(1)}, u32[]{:S(2)}, u32[]{:S(2)}) collective-permute-start(bf16[24,768]{1,0:T(8,128)(2,1)S(1)} %select_convert_fusion.2), channel_id=1, source_target_pairs={{0,64},{64,0},{1,65},{65,1},{2,66},{66,2},{3,67},{67,3},{4,68},{68... | collective-permute-start | bytes 110600 | tf_op jit(solution)/shard_map/ppermute | solution.py:17
  549.1 4.1 collective-permute-start.17
  549.3 7.7 %collective-permute-start.21 = (f32[12,768]{1,0:T(8,128)S(1)}, f32[12,768]{1,0:T(8,128)S(1)}, u32[]{:S(2)}, u32[]{:S(2)}) collective-permute-start(f32[12,768]{1,0:T(8,128)S(1)} %slice_select_fusion.4), channel_id=1, source_target_pairs={{0,2},{2,0},{1,3},{3,1},{4,6},{6,4},{5,7},{7,5},{8,10},{10,8},{9,1... | collective-permute-start | bytes 110600 | tf_op jit(solution)/shard_map/ppermute | solution.py:17
  553.3 4.6 collective-permute-start.18
  569.1 3.7 collective-permute-start.23
  572.9 7.5 %collective-permute-start.24 = (f32[12,2304]{1,0:T(8,128)S(1)}, f32[12,2304]{1,0:T(8,128)S(1)}, u32[]{:S(2)}, u32[]{:S(2)}) collective-permute-start(f32[12,2304]{1,0:T(8,128)S(1)} %slice_select_fusion), channel_id=1, source_target_pairs={{0,2},{2,0},{1,3},{3,1},{4,6},{6,4},{5,7},{7,5},{8,10},{10,8},{9,1... | collective-permute-start | bytes 331784 | tf_op jit(solution)/shard_map/ppermute | solution.py:17
  (81 other events, 322.1 us)
Sparse Core Ops, SparseCore 0:
  21.0 67.8 all-gather.2
